TPU v7x, 256 devices: a whole 4x4x8 slice. The times are simulated.
256 devices in a mesh: hx: 32 (over x, z), hy: 8 (over y, core).
Axes of the slice: x: 4, y: 4, z: 8, core: 2. Of those that a mesh axis runs over, the one named last changes fastest.
Arguments:
- fine_mult: bfloat16 [152, 131072], P(None, ('hx', 'hy')), may hold values from -6 to 6
- up_operators: bfloat16 [8, 152, 152], replicated, may hold values from -0.15625 to 0.15625
- far_operators: bfloat16 [160, 152, 152], replicated, may hold values from -0.0546875 to 0.0546875
- far_list: int32 [160, 131072], P(None, ('hx', 'hy')), may hold values from -1 to 4607, as said below
- ghost_list: int32 [256, 8, 512], P(('hx', 'hy')), may hold values from -1 to 511, as said below
- coarse_list: int32 [160, 32], replicated, may hold values from -1 to 31
Outputs:
- fine_check: float32 [152, 131072], P(None, ('hx', 'hy'))
- coarse_check: float32 [152, 32], replicated
Inputs may be any that keep to these rules, and one draw needn't show every extreme that they name: `far_list`: -1 means no source; a value below 512 is a box of the target's own device; a value 512 + s * 512 + j names slot j of row s of the own device's ghost_list, and that slot is never -1. ghost_list[d, s] holds distinct box numbers local to device d XOR 2**s, followed by -1; for each s some device lists all 512 boxes. `coarse_list`: -1 means no source.
All inputs are finite; a program needn't handle non-finite values.
Results may differ from a plain program's by a relative error of at most 0.009.
Values may be sent and summed in bfloat16 or wider, within the bound.
No kernel may reach another device: no remote copies, remote signals or barrier semaphores. Data moves between devices by JAX's collectives and lax.ppermute only.
A program may use at most 128 MiB of HBM per device.

v0:
```python
import jax
import jax.numpy as jnp
from jax import lax
from jax.sharding import PartitionSpec as P

LEVELS = 3


offset_block = 32


def from_partner(value, axis, stride):
    mask = 2**stride
    pairs = [(source, source ^ mask) for source in range(lax.axis_size(axis))]
    return lax.ppermute(value, axis, pairs)


def translate(source_rows, operators, lists):
    surface = operators.shape[1]
    targets = lists.shape[1]
    groups = lists.shape[0] // offset_block
    operator_blocks = operators.reshape(groups, offset_block, surface, surface)
    list_blocks = lists.reshape(groups, offset_block, targets)

    def add_block(running, pieces):
        block_ops, block_list = pieces
        live_mask = block_list >= 0
        safe_index = jnp.where(live_mask, block_list, 0)
        picked = jnp.take(source_rows, safe_index.reshape(-1), axis=0).reshape(
            offset_block, targets, surface
        )
        picked = picked * live_mask.astype(source_rows.dtype)[:, :, None]
        running = running + jnp.einsum(
            "opq,otq->pt", block_ops, picked, preferred_element_type=jnp.float32
        )
        return (running, None)

    zero_total = jnp.zeros((surface, targets), jnp.float32)
    return lax.scan(add_block, zero_total, (operator_blocks, list_blocks))[0]


def upward(multipoles, operators):
    surface, count = multipoles.shape
    children = multipoles.reshape(surface, count // 8, 8)
    return jnp.einsum("cpq,qnc->pn", operators, children, preferred_element_type=jnp.float32)


def pick_rows(table_rows, index_row, marker):
    live_mask = marker >= 0
    safe_index = jnp.where(live_mask, index_row, 0)
    return jnp.take(table_rows, safe_index, axis=0) * live_mask.astype(table_rows.dtype)[:, None]


def shards(fine_mult, up_operators, far_operators, far_list, ghost_list, coarse_list):
    bits_y = lax.axis_size("hy").bit_length() - 1
    bits_x = lax.axis_size("hx").bit_length() - 1
    own_rows = jnp.transpose(fine_mult)
    wanted = ghost_list[0]
    blocks = []
    for bit_number in range(bits_y):
        requested = from_partner(wanted[bit_number], "hy", bit_number)
        blocks.append(from_partner(pick_rows(own_rows, requested, requested), "hy", bit_number))
    for bit_number in range(bits_x):
        requested = from_partner(wanted[bits_y + bit_number], "hx", bit_number)
        blocks.append(from_partner(pick_rows(own_rows, requested, requested), "hx", bit_number))
    source_rows = jnp.concatenate([own_rows] + blocks, axis=0)
    fine_check = translate(source_rows, far_operators, far_list)
    multipoles = fine_mult
    for level_step in range(LEVELS):
        multipoles = upward(multipoles, up_operators).astype(jnp.bfloat16)
    device_number = lax.axis_index(("hx", "hy"))
    child_op = lax.dynamic_index_in_dim(up_operators, device_number % 8, 0, keepdims=False)
    coarse_term = jnp.dot(child_op, multipoles, preferred_element_type=jnp.float32)
    coarse_boxes = coarse_list.shape[1]
    placement = (jnp.arange(coarse_boxes) == device_number // 8).astype(jnp.float32)
    partial_sum = coarse_term * placement[None, :]
    coarse = lax.psum(partial_sum, ("hx", "hy")).astype(jnp.bfloat16)
    coarse_check = translate(jnp.transpose(coarse), far_operators, coarse_list)
    return (fine_check, coarse_check)


def solution(mesh):
    placed = (
        P(None, ("hx", "hy")),
        P(),
        P(),
        P(None, ("hx", "hy")),
        P(("hx", "hy"), None, None),
        P(),
    )
    return jax.shard_map(
        shards, mesh=mesh, in_specs=placed, out_specs=(P(None, ("hx", "hy")), P()), check_vma=False
    )
```

profile of v0, /device:TPU:1, one launch (start us, length us, event | category | flops | bytes accessed | tf_op | source)
XLA Modules:
  0.0 618.4 jit_solution(17830615330114914494)
XLA Ops:
  0.6 1.6 fusion.33
  2.3 7.8 %collective-permute-start.10 = (s32[512]{0:T(512)}, s32[512]{0:T(512)}, u32[]{:S(2)}, u32[]{:S(2)}) collective-permute-start(s32[512]{0:T(512)} %bitcast.8), channel_id=1, source_target_pairs={{0,32},{8,40},{16,48},{24,56},{32,0},{40,8},{48,16},{56,24},{64,96... | collective-permute-start | bytes 6152 | tf_op jit(solution)/shard_map/ppermute | solution.py:15
  10.1 2.7 collective-permute-start.14
  12.8 1.2 collective-permute-start.8
  14.8 2.9 collective-permute-start.4
  17.7 0.9 copy.16
  18.5 1.0 copy.15
  20.7 73.3 %psum.7 = bf16[152,32]{0,1:T(8,128)(2,1)S(1)} all-reduce(f32[152,32]{0,1:T(8,128)S(1)} %broadcast_multiply_fusion), channel_id=1, replica_groups=mesh['hx'=32,'hy'=8] {'hx','hy'}, use_global_device_ids=true, to_apply=%region_2.4 | all-reduce | flops 4864 | bytes 29184 | tf_op jit(solution)/shard_map/psum | solution.py:77
  94.0 19.8 %copy.14 = bf16[160,152,152]{2,1,0:T(8,128)(2,1)} copy(bf16[160,152,152]{0,2,1:T(8,128)(2,1)} %param.14) | data formatting | bytes 14786560 | tf_op args[2]
  113.8 39.1 %while.23 = (s32[]{:T(128)}, f32[152,32]{0,1:T(8,128)}, bf16[5,32,152,152]{3,2,1,0:T(8,128)(2,1)}, s32[5,32,32]{2,1,0:T(8,128)S(1)}, bf16[32,152]{1,0:T(8,128)(2,1)S(1)}, /*index=5*/s32[]{:T(128)}, s32[]{:T(128)}) while((s32[]{:T(128)}, f32[152,32]{0,1:T(8,128)}, bf16[5,32,152,152]{3,2,1,0:T(8,128)(2,1)}, ...), condition=%wide.region_4.6_spmd.clone, body=%wide.region_3.5_spmd.clone.sunk | while | flops 47654400 | bytes 4152423 | solution.py:39
  114.1 3.9 gather_fusion.1
  118.4 3.2 fusion.53
  121.9 3.9 gather_fusion.1
  126.2 3.2 fusion.53
  129.7 3.9 gather_fusion.1
  134.0 3.2 fusion.53
  137.5 3.9 gather_fusion.1
  141.8 3.2 fusion.53
  145.3 3.9 gather_fusion.1
  149.6 3.2 fusion.53
  154.3 1.0 collective-permute-start
  161.0 2.7 gather_fusion.9
  163.7 2.7 gather_fusion.8
  166.4 2.7 gather_fusion.7
  169.1 2.7 gather_fusion.6
  171.8 2.7 gather_fusion.5
  174.5 2.7 gather_fusion.4
  177.9 1.3 pad_clamp_fusion.6
  179.2 2.7 gather_fusion.3
  181.9 2.7 gather_fusion.2
  185.4 1.1 select_multiply_fusion.9
  187.3 1.1 select_multiply_fusion.8
  188.4 1.8 collective-permute-start.3
  191.0 1.1 select_multiply_fusion.7
  192.1 1.5 collective-permute-start.5
  194.3 1.1 select_multiply_fusion.6
  195.5 1.9 collective-permute-start.7
  198.0 1.1 select_multiply_fusion.5
  201.3 3.3 collective-permute-start.11
  204.6 1.1 collective-permute-start.13
  205.7 0.9 collective-permute-start.15
  206.7 17.8 %collective-permute-done.9 = bf16[512,152]{1,0:T(8,128)(2,1)S(1)} collective-permute-done((bf16[512,152]{1,0:T(8,128)(2,1)S(1)}, bf16[512,152]{1,0:T(8,128)(2,1)S(1)}, u32[]{:S(2)}, u32[]{:S(2)}) %collective-permute-start.9) | collective-permute-done | bytes 155680 | tf_op jit(solution)/shard_map/ppermute | solution.py:15
  224.6 393.1 %while.22 = (s32[]{:T(128)}, f32[152,512]{1,0:T(8,128)S(1)}, bf16[5,32,152,152]{3,2,1,0:T(8,128)(2,1)}, s32[5,32,512]{2,1,0:T(8,128)}, bf16[4608,152]{1,0:T(8,128)(2,1)S(1)}, /*index=5*/s32[]{:T(128)}, s32[]{:T(128)}) while((s32[]{:T(128)}, f32[152,512]{1,0:T(8,128)S(1)}, bf16[5,32,152,152]{3,2,1,0:T(8,128)(2,1)}, ...), condition=%wide.region_1.3_spmd.clone, body=%wide.region_0.2_spmd.clone.sunk | while | flops 762454016 | bytes 28868712 | solution.py:39
  224.7 0.9 fusion.49
  226.6 65.2 %gather_fusion = bf16[16384,152]{1,0:T(8,128)(2,1)} fusion(bf16[4608,152]{1,0:T(8,128)(2,1)S(1)} %get-tuple-element.239, s32[16384]{0:T(1024)S(1)} %broadcast_clamp_fusion.4), kind=kCustom, calls=%fused_computation.1.clone.clone.1 | custom fusion | bytes 10027008 | tf_op jit(solution)/shard_map/while/body/eval_jaxpr/jit(_take)/gather | solution.py:29
  291.8 6.7 %select_multiply_fusion.12 = bf16[16384,152]{1,0:T(8,128)(2,1)S(1)} fusion(bf16[16384,152]{1,0:T(8,128)(2,1)} %gather_fusion, pred[16384]{0:T(1024)(128)(4,1)S(1)} %bitcast.146, bf16[16384]{0:T(1024)(128)(2,1)S(1)} %bitcast.145), kind=kLoop, calls=%fused_computation.10.clone.1 | loop fusion | flops 4980736 | bytes 10010624 | tf_op jit(solution)/shard_map/while/body/eval_jaxpr/mul | solution.py:32
  298.5 4.7 fusion.50
  303.3 0.9 fusion.49
  304.2 0.9 dynamic-slice_bitcast_fusion.2
  305.2 65.2 %gather_fusion = bf16[16384,152]{1,0:T(8,128)(2,1)} fusion(bf16[4608,152]{1,0:T(8,128)(2,1)S(1)} %get-tuple-element.239, s32[16384]{0:T(1024)S(1)} %broadcast_clamp_fusion.4), kind=kCustom, calls=%fused_computation.1.clone.clone.1 | custom fusion | bytes 10027008 | tf_op jit(solution)/shard_map/while/body/eval_jaxpr/jit(_take)/gather | solution.py:29
  370.4 6.7 %select_multiply_fusion.12 = bf16[16384,152]{1,0:T(8,128)(2,1)S(1)} fusion(bf16[16384,152]{1,0:T(8,128)(2,1)} %gather_fusion, pred[16384]{0:T(1024)(128)(4,1)S(1)} %bitcast.146, bf16[16384]{0:T(1024)(128)(2,1)S(1)} %bitcast.145), kind=kLoop, calls=%fused_computation.10.clone.1 | loop fusion | flops 4980736 | bytes 10010624 | tf_op jit(solution)/shard_map/while/body/eval_jaxpr/mul | solution.py:32
  377.1 4.7 fusion.50
  381.9 0.9 fusion.49
  383.9 65.2 %gather_fusion = bf16[16384,152]{1,0:T(8,128)(2,1)} fusion(bf16[4608,152]{1,0:T(8,128)(2,1)S(1)} %get-tuple-element.239, s32[16384]{0:T(1024)S(1)} %broadcast_clamp_fusion.4), kind=kCustom, calls=%fused_computation.1.clone.clone.1 | custom fusion | bytes 10027008 | tf_op jit(solution)/shard_map/while/body/eval_jaxpr/jit(_take)/gather | solution.py:29
  449.0 6.7 %select_multiply_fusion.12 = bf16[16384,152]{1,0:T(8,128)(2,1)S(1)} fusion(bf16[16384,152]{1,0:T(8,128)(2,1)} %gather_fusion, pred[16384]{0:T(1024)(128)(4,1)S(1)} %bitcast.146, bf16[16384]{0:T(1024)(128)(2,1)S(1)} %bitcast.145), kind=kLoop, calls=%fused_computation.10.clone.1 | loop fusion | flops 4980736 | bytes 10010624 | tf_op jit(solution)/shard_map/while/body/eval_jaxpr/mul | solution.py:32
  455.7 4.7 fusion.50
  460.5 0.9 fusion.49
  462.5 65.2 %gather_fusion = bf16[16384,152]{1,0:T(8,128)(2,1)} fusion(bf16[4608,152]{1,0:T(8,128)(2,1)S(1)} %get-tuple-element.239, s32[16384]{0:T(1024)S(1)} %broadcast_clamp_fusion.4), kind=kCustom, calls=%fused_computation.1.clone.clone.1 | custom fusion | bytes 10027008 | tf_op jit(solution)/shard_map/while/body/eval_jaxpr/jit(_take)/gather | solution.py:29
  527.6 6.7 %select_multiply_fusion.12 = bf16[16384,152]{1,0:T(8,128)(2,1)S(1)} fusion(bf16[16384,152]{1,0:T(8,128)(2,1)} %gather_fusion, pred[16384]{0:T(1024)(128)(4,1)S(1)} %bitcast.146, bf16[16384]{0:T(1024)(128)(2,1)S(1)} %bitcast.145), kind=kLoop, calls=%fused_computation.10.clone.1 | loop fusion | flops 4980736 | bytes 10010624 | tf_op jit(solution)/shard_map/while/body/eval_jaxpr/mul | solution.py:32
  534.3 4.7 fusion.50
  539.1 0.9 fusion.49
  541.1 65.2 %gather_fusion = bf16[16384,152]{1,0:T(8,128)(2,1)} fusion(bf16[4608,152]{1,0:T(8,128)(2,1)S(1)} %get-tuple-element.239, s32[16384]{0:T(1024)S(1)} %broadcast_clamp_fusion.4), kind=kCustom, calls=%fused_computation.1.clone.clone.1 | custom fusion | bytes 10027008 | tf_op jit(solution)/shard_map/while/body/eval_jaxpr/jit(_take)/gather | solution.py:29
  606.3 6.7 %select_multiply_fusion.12 = bf16[16384,152]{1,0:T(8,128)(2,1)S(1)} fusion(bf16[16384,152]{1,0:T(8,128)(2,1)} %gather_fusion, pred[16384]{0:T(1024)(128)(4,1)S(1)} %bitcast.146, bf16[16384]{0:T(1024)(128)(2,1)S(1)} %bitcast.145), kind=kLoop, calls=%fused_computation.10.clone.1 | loop fusion | flops 4980736 | bytes 10010624 | tf_op jit(solution)/shard_map/while/body/eval_jaxpr/mul | solution.py:32
  613.0 4.7 fusion.50
  (146 shorter events, 23.7 us)
Async XLA Ops:
  0.6 19.0 %copy-start = (bf16[8,152,152]{2,1,0:T(8,128)(2,1)S(1)}, bf16[8,152,152]{2,1,0:T(8,128)(2,1)}, u32[]{:S(2)}) copy-start(bf16[8,152,152]{2,1,0:T(8,128)(2,1)} %param.13) | copy-start | bytes 1108996
  2.3 150.6 %collective-permute-start.10 = (s32[512]{0:T(512)}, s32[512]{0:T(512)}, u32[]{:S(2)}, u32[]{:S(2)}) collective-permute-start(s32[512]{0:T(512)} %bitcast.8), channel_id=1, source_target_pairs={{0,32},{8,40},{16,48},{24,56},{32,0},{40,8},{48,16},{56,24},{64,96... | collective-permute-start | bytes 6152 | tf_op jit(solution)/shard_map/ppermute | solution.py:15
  10.1 144.2 %collective-permute-start.14 = (s32[512]{0:T(512)}, s32[512]{0:T(512)}, u32[]{:S(2)}, u32[]{:S(2)}) collective-permute-start(s32[512]{0:T(512)} %bitcast.10), channel_id=1, source_target_pairs={{0,128},{8,136},{16,144},{24,152},{32,160},{40,168},{48,176},{56,1... | collective-permute-start | bytes 6152 | tf_op jit(solution)/shard_map/ppermute | solution.py:15
  12.8 143.1 %collective-permute-start.8 = (s32[512]{0:T(512)}, s32[512]{0:T(512)}, u32[]{:S(2)}, u32[]{:S(2)}) collective-permute-start(s32[512]{0:T(512)} %bitcast.7), channel_id=1, source_target_pairs={{0,16},{8,24},{16,0},{24,8},{32,48},{40,56},{48,32},{56,40},{64,80... | collective-permute-start | bytes 6152 | tf_op jit(solution)/shard_map/ppermute | solution.py:15
  14.0 142.6 %collective-permute-start.6 = (s32[512]{0:T(512)}, s32[512]{0:T(512)}, u32[]{:S(2)}, u32[]{:S(2)}) collective-permute-start(s32[512]{0:T(512)} %bitcast.6), channel_id=1, source_target_pairs={{0,8},{8,0},{16,24},{24,16},{32,40},{40,32},{48,56},{56,48},{64,72... | collective-permute-start | bytes 6152 | tf_op jit(solution)/shard_map/ppermute | solution.py:15
  14.8 142.5 %collective-permute-start.4 = (s32[512]{0:T(512)}, s32[512]{0:T(512)}, u32[]{:S(2)}, u32[]{:S(2)}) collective-permute-start(s32[512]{0:T(512)} %bitcast.5), channel_id=1, source_target_pairs={{0,4},{1,5},{2,6},{3,7},{4,0},{5,1},{6,2},{7,3},{8,12},{9,13},{10,... | collective-permute-start | bytes 6152 | tf_op jit(solution)/shard_map/ppermute | solution.py:15
  152.9 5.7 collective-permute-start.2
  154.3 22.9 %collective-permute-start = (s32[512]{0:T(512)}, s32[512]{0:T(512)}, u32[]{:S(2)}, u32[]{:S(2)}) collective-permute-start(s32[512]{0:T(512)} %bitcast.151), channel_id=1, source_target_pairs={{0,1},{1,0},{2,3},{3,2},{4,5},{5,4},{6,7},{7,6},{8,9},{9,8},{10,11... | collective-permute-start | bytes 6152 | tf_op jit(solution)/shard_map/ppermute | solution.py:15
  155.9 3.9 collective-permute-start.12
  158.6 1.7 copy-start.7
  159.8 0.5 copy-start.5
  184.6 15.3 %copy-start.4 = (bf16[512,152]{1,0:T(8,128)(2,1)S(1)}, bf16[512,152]{1,0:T(8,128)(2,1)}, u32[]{:S(2)}) copy-start(bf16[512,152]{1,0:T(8,128)(2,1)} %gather_fusion.9) | copy-start | bytes 466948
  184.6 15.5 %copy-start.6 = (s32[512]{0:T(512)S(1)}, s32[512]{0:T(512)}, u32[]{:S(2)}) copy-start(s32[512]{0:T(512)} %copy-done.5) | copy-start | bytes 6148
  184.6 15.5 %copy-start.3 = (bf16[512,152]{1,0:T(8,128)(2,1)S(1)}, bf16[512,152]{1,0:T(8,128)(2,1)}, u32[]{:S(2)}) copy-start(bf16[512,152]{1,0:T(8,128)(2,1)} %gather_fusion.8) | copy-start | bytes 466948
  184.6 16.4 %copy-start.2 = (bf16[512,152]{1,0:T(8,128)(2,1)S(1)}, bf16[512,152]{1,0:T(8,128)(2,1)}, u32[]{:S(2)}) copy-start(bf16[512,152]{1,0:T(8,128)(2,1)} %gather_fusion.7) | copy-start | bytes 466948
  186.6 14.7 %collective-permute-start.1 = (bf16[512,152]{1,0:T(8,128)(2,1)S(1)}, bf16[512,152]{1,0:T(8,128)(2,1)S(1)}, u32[]{:S(2)}, u32[]{:S(2)}) collective-permute-start(bf16[512,152]{1,0:T(8,128)(2,1)S(1)} %select_multiply_fusion.9), channel_id=1, source_target_pairs={{0,1},{1,0},{2,3},{3,2},{4,5},{5,4},{6,7},{7,6},{8,9},{9,8},{10,11... | collective-permute-start | bytes 466952 | tf_op jit(solution)/shard_map/ppermute | solution.py:15
  188.4 16.2 %collective-permute-start.3 = (bf16[512,152]{1,0:T(8,128)(2,1)S(1)}, bf16[512,152]{1,0:T(8,128)(2,1)S(1)}, u32[]{:S(2)}, u32[]{:S(2)}) collective-permute-start(bf16[512,152]{1,0:T(8,128)(2,1)S(1)} %select_multiply_fusion.8), channel_id=1, source_target_pairs={{0,2},{1,3},{2,0},{3,1},{4,6},{5,7},{6,4},{7,5},{8,10},{9,11},{10,... | collective-permute-start | bytes 466952 | tf_op jit(solution)/shard_map/ppermute | solution.py:15
  192.1 13.6 %collective-permute-start.5 = (bf16[512,152]{1,0:T(8,128)(2,1)S(1)}, bf16[512,152]{1,0:T(8,128)(2,1)S(1)}, u32[]{:S(2)}, u32[]{:S(2)}) collective-permute-start(bf16[512,152]{1,0:T(8,128)(2,1)S(1)} %select_multiply_fusion.7), channel_id=1, source_target_pairs={{0,4},{1,5},{2,6},{3,7},{4,0},{5,1},{6,2},{7,3},{8,12},{9,13},{10,... | collective-permute-start | bytes 466952 | tf_op jit(solution)/shard_map/ppermute | solution.py:15
  195.5 11.2 %collective-permute-start.7 = (bf16[512,152]{1,0:T(8,128)(2,1)S(1)}, bf16[512,152]{1,0:T(8,128)(2,1)S(1)}, u32[]{:S(2)}, u32[]{:S(2)}) collective-permute-start(bf16[512,152]{1,0:T(8,128)(2,1)S(1)} %select_multiply_fusion.6), channel_id=1, source_target_pairs={{0,8},{8,0},{16,24},{24,16},{32,40},{40,32},{48,56},{56,48},{64,72... | collective-permute-start | bytes 466952 | tf_op jit(solution)/shard_map/ppermute | solution.py:15
  199.2 25.3 %collective-permute-start.9 = (bf16[512,152]{1,0:T(8,128)(2,1)S(1)}, bf16[512,152]{1,0:T(8,128)(2,1)S(1)}, u32[]{:S(2)}, u32[]{:S(2)}) collective-permute-start(bf16[512,152]{1,0:T(8,128)(2,1)S(1)} %select_multiply_fusion.5), channel_id=1, source_target_pairs={{0,16},{8,24},{16,0},{24,8},{32,48},{40,56},{48,32},{56,40},{64,80... | collective-permute-start | bytes 466952 | tf_op jit(solution)/shard_map/ppermute | solution.py:15
  201.3 23.3 %collective-permute-start.11 = (bf16[512,152]{1,0:T(8,128)(2,1)S(1)}, bf16[512,152]{1,0:T(8,128)(2,1)S(1)}, u32[]{:S(2)}, u32[]{:S(2)}) collective-permute-start(bf16[512,152]{1,0:T(8,128)(2,1)S(1)} %select_multiply_fusion.4), channel_id=1, source_target_pairs={{0,32},{8,40},{16,48},{24,56},{32,0},{40,8},{48,16},{56,24},{64,96... | collective-permute-start | bytes 466952 | tf_op jit(solution)/shard_map/ppermute | solution.py:15
  204.6 19.9 %collective-permute-start.13 = (bf16[512,152]{1,0:T(8,128)(2,1)S(1)}, bf16[512,152]{1,0:T(8,128)(2,1)S(1)}, u32[]{:S(2)}, u32[]{:S(2)}) collective-permute-start(bf16[512,152]{1,0:T(8,128)(2,1)S(1)} %select_multiply_fusion.3), channel_id=1, source_target_pairs={{0,64},{8,72},{16,80},{24,88},{32,96},{40,104},{48,112},{56,120},{... | collective-permute-start | bytes 466952 | tf_op jit(solution)/shard_map/ppermute | solution.py:15
  205.7 18.9 %collective-permute-start.15 = (bf16[512,152]{1,0:T(8,128)(2,1)S(1)}, bf16[512,152]{1,0:T(8,128)(2,1)S(1)}, u32[]{:S(2)}, u32[]{:S(2)}) collective-permute-start(bf16[512,152]{1,0:T(8,128)(2,1)S(1)} %select_multiply_fusion.2), channel_id=1, source_target_pairs={{0,128},{8,136},{16,144},{24,152},{32,160},{40,168},{48,176},{56,1... | collective-permute-start | bytes 466952 | tf_op jit(solution)/shard_map/ppermute | solution.py:15
  617.7 0.7 copy-start.1
where the time goes:
time: 621 us; the launch traced here: 618 us
  local copies, waits for them, and re-layouts  398 us (64%)
  blocking collectives  73.3 us (12%)
  other arithmetic  59.2 us (10%)
  matrix products  40.7 us (7%)
  starting transfers between devices  27.9 us (4%)
  waiting for transfers between devices  17.9 us (3%)
    gather x10, local copies, waits for them, and re-layouts, add_block(): jnp.take(source_rows, safe_index.reshape(-1), axis=0)  346 us
    psum x1, blocking collectives, shards(): coarse = lax.psum(partial_sum, ('hx', 'hy')).astype(jnp.bfloat16)  73.3 us
    dot_general x10, matrix products, add_block(): jnp.einsum('opq,otq->pt', block_ops, picked, preferred_element_type=jnp.f...  39.7 us
    mul x15, other arithmetic, add_block(): picked = picked * live_mask.astype(source_rows.dtype)[:, :, None]  35.2 us
    ppermute x16, starting transfers between devices, from_partner(): return lax.ppermute(value, axis, pairs)  27.9 us
    unnamed x27, local copies, waits for them, and re-layouts  23.1 us
    gather x8, local copies, waits for them, and re-layouts, pick_rows(): jnp.take(table_rows, safe_index, axis=0)  21.7 us
    ppermute x16, waiting for transfers between devices, from_partner(): return lax.ppermute(value, axis, pairs)  17.9 us
  transfers between devices with their start and end apart: 16, of which 1 were waited for; matrix products, arithmetic and copies ran while one was open for 15% of the time, Pallas kernels for 0%

commit v1 on v0

v1 whole, which is shorter than its diff:
```python
import functools

import jax
import jax.numpy as jnp
from jax import lax
from jax.experimental import pallas as pl
from jax.experimental.pallas import tpu as pltpu
from jax.sharding import PartitionSpec as P

LEVELS = 3
LANES = 128
NT = (((1,), (1,)), ((), ()))


def from_partner(value, axis, stride):
    mask = 2**stride
    pairs = [(source, source ^ mask) for source in range(lax.axis_size(axis))]
    return lax.ppermute(value, axis, pairs)


def lift(rows, up_ref):
    surface = up_ref.shape[1]
    count = rows.shape[1] // 8
    total = None
    for octant in range(8):
        children = jnp.concatenate([rows[half, pl.ds(octant, count, stride=8), :] for half in range(2)], axis=1)
        children = children[:, :surface].astype(jnp.bfloat16)
        term = lax.dot_general(children, up_ref[octant], NT, preferred_element_type=jnp.float32)
        total = term if total is None else total + term
    return total


def upward_kernel(fine_ref, up_ref, out_ref, *levels):
    surface, boxes = fine_ref.shape
    spot = lax.broadcasted_iota(jnp.int32, (boxes, boxes), 0) == lax.broadcasted_iota(jnp.int32, (boxes, boxes), 1)
    rows = lax.dot_general(
        spot.astype(jnp.float32).astype(jnp.bfloat16), fine_ref[...], NT, preferred_element_type=jnp.float32
    )
    for level in levels:
        level[0] = rows[:, :LANES]
        level[1, :, : surface - LANES] = rows[:, LANES:]
        rows = lift(level, up_ref).astype(jnp.bfloat16).astype(jnp.float32)
    out_ref[...] = rows


def upward(fine_mult, up_operators):
    surface, boxes = fine_mult.shape
    return pl.pallas_call(
        upward_kernel,
        out_shape=jax.ShapeDtypeStruct((boxes // 8**LEVELS, surface), jnp.float32),
        scratch_shapes=[pltpu.VMEM((2, boxes // 8**level, LANES), jnp.float32) for level in range(LEVELS)],
        name="upward",
    )(fine_mult, up_operators)


def translate_kernel(sections, idx_hbm, slots_ref, poles_ref, up_ref, far_ref, *rest):
    blocks = rest[:sections]
    fine_out, coarse_out, table, buf_a, buf_b, acc, poles, idx_a, idx_b, sem = rest[sections:]
    step = pl.program_id(0)
    pairs = pl.num_programs(0) - 1
    surface = far_ref.shape[1]
    boxes = blocks[0].shape[1]
    targets = acc.shape[0]
    tail = surface - LANES

    def fetch(pair, where, slot):
        return [
            pltpu.make_async_copy(idx_hbm.at[2 * pair + k], where.at[k], sem.at[slot, k]) for k in range(2)
        ]

    def put(first, rows):
        count = rows.shape[0]
        table[pl.ds(2 * first, count, stride=2), :] = rows[:, :LANES]
        table[pl.ds(2 * first + 1, count, stride=2), :] = jnp.concatenate(
            [rows[:, LANES:], jnp.zeros((count, LANES - tail), jnp.float32)], axis=1
        )

    def gather(where, buf):
        for k in range(2):
            for target in range(targets):
                buf[k, 2 * target : 2 * target + 2, :] = table[pl.ds(where[k, target], 2), :]

    def multiply(buf):
        rows, weights = [], []
        for k in range(2):
            rows += [buf[k, pl.ds(0, targets, stride=2), :], buf[k, pl.ds(1, targets, stride=2), :]]
            weights += [far_ref[k], jnp.zeros((surface, LANES - tail), jnp.bfloat16)]
        rows = jnp.concatenate([piece.astype(jnp.bfloat16) for piece in rows], axis=1)
        weights = jnp.concatenate(weights, axis=1)
        acc[...] += lax.dot_general(rows, weights, NT, preferred_element_type=jnp.float32)

    @pl.when(step == 0)
    def _():
        for copy in fetch(0, idx_a, 0):
            copy.start()
        acc[...] = jnp.zeros_like(acc)
        number = lax.broadcasted_iota(jnp.int32, (boxes, boxes), 1)
        for section in range(sections):
            spot = (slots_ref[:, section : section + 1] == number).astype(jnp.float32).astype(jnp.bfloat16)
            put(
                section * boxes,
                lax.dot_general(spot, blocks[section][...], NT, preferred_element_type=jnp.float32),
            )
        poles[0] = poles_ref[:, :LANES]
        poles[1, :, :tail] = poles_ref[:, LANES:]
        coarse = lift(poles, up_ref).astype(jnp.bfloat16).astype(jnp.float32)
        put(sections * boxes, coarse)
        put(sections * boxes + coarse.shape[0], jnp.zeros((8, surface), jnp.float32))

    even = step % 2 == 0

    @pl.when(jnp.logical_and(even, step < pairs))
    def _():
        for copy in fetch(step, idx_a, 0):
            copy.wait()
        for copy in fetch(step + 1, idx_b, 1):
            copy.start()

    @pl.when(jnp.logical_not(even))
    def _():
        for copy in fetch(step, idx_b, 1):
            copy.wait()

    @pl.when(jnp.logical_and(jnp.logical_not(even), step < pairs - 1))
    def _():
        for copy in fetch(step + 1, idx_a, 0):
            copy.start()

    @pl.when(step == 0)
    def _():
        gather(idx_a, buf_a)

    @pl.when(jnp.logical_and(even, jnp.logical_and(step > 0, step < pairs)))
    def _():
        gather(idx_a, buf_a)
        multiply(buf_b)

    @pl.when(jnp.logical_not(even))
    def _():
        gather(idx_b, buf_b)
        multiply(buf_a)

    @pl.when(step == pairs)
    def _():
        multiply(buf_b)
        fine_out[...] = jnp.transpose(acc[:boxes, :])
        coarse_out[...] = acc[boxes:, :]


def translate(idx, slots, poles, up_operators, far_operators, blocks):
    offsets, targets = idx.shape
    surface, boxes = blocks[0].shape
    sections = len(blocks)
    coarse = targets - boxes
    rows = sections * boxes + coarse + 8
    whole = lambda *shape: pl.BlockSpec(shape, lambda step: (0,) * len(shape))
    return pl.pallas_call(
        functools.partial(translate_kernel, sections),
        grid=(offsets // 2 + 1,),
        in_specs=[
            pl.BlockSpec(memory_space=pl.ANY),
            whole(*slots.shape),
            whole(*poles.shape),
            whole(*up_operators.shape),
            pl.BlockSpec((2, surface, surface), lambda step: (jnp.maximum(step - 1, 0), 0, 0)),
        ]
        + [whole(surface, boxes) for _ in blocks],
        out_specs=[whole(surface, boxes), whole(coarse, surface)],
        out_shape=[
            jax.ShapeDtypeStruct((surface, boxes), jnp.float32),
            jax.ShapeDtypeStruct((coarse, surface), jnp.float32),
        ],
        scratch_shapes=[
            pltpu.VMEM((2 * rows, LANES), jnp.float32),
            pltpu.VMEM((2, 2 * targets, LANES), jnp.float32),
            pltpu.VMEM((2, 2 * targets, LANES), jnp.float32),
            pltpu.VMEM((targets, surface), jnp.float32),
            pltpu.VMEM((2, poles.shape[0], LANES), jnp.float32),
            pltpu.SMEM((2, targets), jnp.int32),
            pltpu.SMEM((2, targets), jnp.int32),
            pltpu.SemaphoreType.DMA((2, 2)),
        ],
        compiler_params=pltpu.CompilerParams(vmem_limit_bytes=48 << 20),
        name="translate",
    )(idx, slots, poles, up_operators, far_operators, *blocks)


def shards(fine_mult, up_operators, far_operators, far_list, ghost_list, coarse_list):
    surface, boxes = fine_mult.shape
    bits_y = lax.axis_size("hy").bit_length() - 1
    bits_x = lax.axis_size("hx").bit_length() - 1
    blocks = [fine_mult]
    for bit_number in range(bits_y):
        blocks.append(from_partner(fine_mult, "hy", bit_number))
    for bit_number in range(bits_x):
        blocks.append(from_partner(fine_mult, "hx", bit_number))
    sections = len(blocks)
    multipoles = upward(fine_mult, up_operators)
    poles = lax.all_gather(multipoles, ("hx", "hy"), axis=0, tiled=True)
    coarse_boxes = coarse_list.shape[1]
    first_coarse = sections * boxes
    zero_row = first_coarse + coarse_boxes
    idx = jnp.concatenate(
        [
            2 * jnp.where(far_list < 0, zero_row, far_list),
            2 * jnp.where(coarse_list < 0, zero_row, coarse_list + first_coarse),
        ],
        axis=1,
    )
    slots = jnp.concatenate([jnp.arange(boxes, dtype=jnp.int32)[:, None], jnp.transpose(ghost_list[0])], axis=1)
    fine_check, coarse_check = translate(idx, slots, poles, up_operators, far_operators, blocks)
    return (fine_check, jnp.transpose(coarse_check))


def solution(mesh):
    placed = (
        P(None, ("hx", "hy")),
        P(),
        P(),
        P(None, ("hx", "hy")),
        P(("hx", "hy"), None, None),
        P(),
    )
    return jax.shard_map(
        shards, mesh=mesh, in_specs=placed, out_specs=(P(None, ("hx", "hy")), P()), check_vma=False
    )
```

time: 621 us -> 182 us (0.29)
  local copies, waits for them, and re-layouts: 398 us -> 20.8 us
  Pallas kernels: 0 us -> 75.4 us
  other arithmetic: 59.2 us -> 1.78 us
  matrix products: 40.7 us -> 0 us
  waiting for transfers between devices: 17.9 us -> 1.59 us
  blocking collectives: 73.3 us -> 60.3 us
  starting transfers between devices: 27.9 us -> 19.2 us
    gather x18 -> x0, local copies, waits for them, and re-layouts: 367 us -> none  [the longest x10 346 us: add_block(): jnp.take(source_rows, safe_index.reshape(-1), axis=0)]
    pallas_call x0 -> x2, Pallas kernels: none -> 75.4 us  [the longest x1 72 us: translate(): pl.pallas_call(functools.partial(translate_kernel, sections), grid=(offse...]
    psum x1 -> x0, blocking collectives: 73.3 us -> none  [shards(): coarse = lax.psum(partial_sum, ('hx', 'hy')).astype(jnp.bfloat16)]
    all_gather x0 -> x1, blocking collectives: none -> 60.3 us  [shards(): poles = lax.all_gather(multipoles, ('hx', 'hy'), axis=0, tiled=True)]
    dot_general x14 -> x0, matrix products: 40.7 us -> none  [the longest x10 39.7 us: add_block(): jnp.einsum('opq,otq->pt', block_ops, picked, preferred_element_type=jnp.f...]
    mul x24 -> x2, other arithmetic: 41.6 us -> 1.03 us  [the longest x1 1.01 us: shards(): 2 * jnp.where(far_list < 0, zero_row, far_list)]
    ppermute x16 -> x8, waiting for transfers between devices: 17.9 us -> 1.59 us  [from_partner(): return lax.ppermute(value, axis, pairs)]
    ppermute x16 -> x8, starting transfers between devices: 27.9 us -> 19.2 us  [from_partner(): return lax.ppermute(value, axis, pairs)]
  transfers between devices with their start and end apart: 16 -> 8, of which waited for: 1 -> 1; matrix products, arithmetic and copies ran while one was open for 15% -> 13% of each run, Pallas kernels for 0% -> 2%
where the time goes in v1:
time: 182 us; the launch traced here: 180 us
  Pallas kernels  75.4 us (41%)
  blocking collectives  60.3 us (33%)
  local copies, waits for them, and re-layouts  20.8 us (11%)
  starting transfers between devices  19.2 us (11%)
    pallas_call x1, Pallas kernels, translate(): pl.pallas_call(functools.partial(translate_kernel, sections), grid=(offse...  72 us
    all_gather x1, blocking collectives, shards(): poles = lax.all_gather(multipoles, ('hx', 'hy'), axis=0, tiled=True)  60.3 us
    unnamed x7, local copies, waits for them, and re-layouts  20.7 us
    ppermute x8, starting transfers between devices, from_partner(): return lax.ppermute(value, axis, pairs)  19.2 us
  transfers between devices with their start and end apart: 8, of which 1 were waited for; matrix products, arithmetic and copies ran while one was open for 13% of the time, Pallas kernels for 2%

profile of v1, /device:TPU:1, one launch (start us, length us, event | category | flops | bytes accessed | tf_op | source)
XLA Modules:
  0.0 179.8 jit_solution(11790789426839567811)
XLA Ops:
  0.6 2.1 %collective-permute-start.6 = (bf16[152,512]{1,0:T(8,128)(2,1)}, bf16[152,512]{1,0:T(8,128)(2,1)S(1)}, u32[]{:S(2)}, u32[]{:S(2)}) collective-permute-start(bf16[152,512]{1,0:T(8,128)(2,1)} %rest_0_.1), channel_id=1, source_target_pairs={{0,64},{8,72},{16,80},{24,88},{32,96},{40,104},{48,112},{56,120},{... | collective-permute-start | bytes 466952 | tf_op jit(solution)/shard_map/ppermute | solution.py:18
  2.8 6.9 %collective-permute-start.5 = (bf16[152,512]{1,0:T(8,128)(2,1)}, bf16[152,512]{1,0:T(8,128)(2,1)S(1)}, u32[]{:S(2)}, u32[]{:S(2)}) collective-permute-start(bf16[152,512]{1,0:T(8,128)(2,1)} %rest_0_.1), channel_id=1, source_target_pairs={{0,32},{8,40},{16,48},{24,56},{32,0},{40,8},{48,16},{56,24},{64,96... | collective-permute-start | bytes 466952 | tf_op jit(solution)/shard_map/ppermute | solution.py:18
  9.7 1.2 collective-permute-start.4
  10.9 0.7 collective-permute-start.3
  11.6 2.9 %collective-permute-start.2 = (bf16[152,512]{1,0:T(8,128)(2,1)}, bf16[152,512]{1,0:T(8,128)(2,1)S(1)}, u32[]{:S(2)}, u32[]{:S(2)}) collective-permute-start(bf16[152,512]{1,0:T(8,128)(2,1)} %rest_0_.1), channel_id=1, source_target_pairs={{0,4},{1,5},{2,6},{3,7},{4,0},{5,1},{6,2},{7,3},{8,12},{9,13},{10,... | collective-permute-start | bytes 466952 | tf_op jit(solution)/shard_map/ppermute | solution.py:18
  14.5 0.9 copy.16
  15.4 1.0 fusion
  16.4 3.4 %upward.1 = f32[1,152]{1,0:T(1,128)} custom-call(bf16[152,512]{1,0:T(8,128)(2,1)} %rest_0_.1, bf16[8,152,152]{2,1,0:T(8,128)(2,1)} %up_ref.3), custom_call_target="tpu_custom_call" | custom-call | tf_op jit(solution)/shard_map/upward/pallas_call | solution.py:48
  19.8 0.7 pad_add_fusion.1
  20.5 0.0 collective-permute-done.6.rest_7_
  20.5 0.5 collective-permute-start.1
  21.0 0.0 collective-permute-done.5.rest_6_
  21.0 2.4 %collective-permute-start = (bf16[152,512]{1,0:T(8,128)(2,1)}, bf16[152,512]{1,0:T(8,128)(2,1)S(1)}, u32[]{:S(2)}, u32[]{:S(2)}) collective-permute-start(bf16[152,512]{1,0:T(8,128)(2,1)} %rest_0_.1), channel_id=1, source_target_pairs={{0,1},{1,0},{2,3},{3,2},{4,5},{5,4},{6,7},{7,6},{8,9},{9,8},{10,11... | collective-permute-start | bytes 466952 | tf_op jit(solution)/shard_map/ppermute | solution.py:18
  23.4 1.6 collective-permute-done.4.rest_5_
  24.9 2.5 %collective-permute-start.7 = (bf16[152,512]{1,0:T(8,128)(2,1)}, bf16[152,512]{1,0:T(8,128)(2,1)S(1)}, u32[]{:S(2)}, u32[]{:S(2)}) collective-permute-start(bf16[152,512]{1,0:T(8,128)(2,1)} %rest_0_.1), channel_id=1, source_target_pairs={{0,128},{8,136},{16,144},{24,152},{32,160},{40,168},{48,176},{56,1... | collective-permute-start | bytes 466952 | tf_op jit(solution)/shard_map/ppermute | solution.py:18
  27.4 60.3 %all-gather = f32[256,1,152]{2,1,0:T(1,128)S(1)} all-gather(f32[1,1,152]{2,1,0:T(1,128)} %bitcast.11), channel_id=1, replica_groups=mesh['hx'=32,'hy'=8] {'hx','hy'}, dimensions={0}, use_global_device_ids=true | all-gather | bytes 156256 | tf_op jit(solution)/shard_map/all_gather | solution.py:199
  87.7 0.1 copy.19.slots_ref
  87.9 0.0 copy-start
  87.9 0.0 copy-start.1
  87.9 19.8 %copy.21.far_ref = bf16[160,152,152]{2,1,0:T(8,128)(2,1)} copy(bf16[160,152,152]{0,2,1:T(8,128)(2,1)} %param.8) | data formatting | bytes 14786560 | tf_op args[2]
  107.7 0.0 collective-permute-done.3.rest_4_
  107.7 0.0 collective-permute-done.2.rest_3_
  107.7 0.0 collective-permute-done.1.rest_2_
  107.7 0.0 collective-permute-done.rest_1_
  107.8 0.0 collective-permute-done.7.rest_8_
  107.8 0.0 copy-done
  107.8 0.0 copy-done.1
  107.8 72.0 %translate.1 = (f32[152,512]{1,0:T(8,128)}, f32[32,152]{1,0:T(8,128)}) custom-call(s32[160,544]{1,0:T(8,128)S(1)} %pad_add_fusion.idx_hbm, s32[512,9]{1,0:T(8,128)S(1)} %copy.19.slots_ref, f32[256,152]{1,0:T(8,128)S(1)} %bitcast.9, bf16[8,152,152]{2,1,0:T(8,128)(2,1)S(1)} %copy-done, bf16[160,152,152]{2,1,0:T(8,128)(2,1)} %copy.21.far_ref, ...), custom_call_target="tpu_custom_call" | custom-call | tf_op jit(solution)/shard_map/translate/pallas_call | solution.py:157
  (4 shorter events, 0.1 us)
Async XLA Ops:
  0.6 19.9 %collective-permute-start.6 = (bf16[152,512]{1,0:T(8,128)(2,1)}, bf16[152,512]{1,0:T(8,128)(2,1)S(1)}, u32[]{:S(2)}, u32[]{:S(2)}) collective-permute-start(bf16[152,512]{1,0:T(8,128)(2,1)} %rest_0_.1), channel_id=1, source_target_pairs={{0,64},{8,72},{16,80},{24,88},{32,96},{40,104},{48,112},{56,120},{... | collective-permute-start | bytes 466952 | tf_op jit(solution)/shard_map/ppermute | solution.py:18
  2.8 18.3 %collective-permute-start.5 = (bf16[152,512]{1,0:T(8,128)(2,1)}, bf16[152,512]{1,0:T(8,128)(2,1)S(1)}, u32[]{:S(2)}, u32[]{:S(2)}) collective-permute-start(bf16[152,512]{1,0:T(8,128)(2,1)} %rest_0_.1), channel_id=1, source_target_pairs={{0,32},{8,40},{16,48},{24,56},{32,0},{40,8},{48,16},{56,24},{64,96... | collective-permute-start | bytes 466952 | tf_op jit(solution)/shard_map/ppermute | solution.py:18
  9.7 15.3 %collective-permute-start.4 = (bf16[152,512]{1,0:T(8,128)(2,1)}, bf16[152,512]{1,0:T(8,128)(2,1)S(1)}, u32[]{:S(2)}, u32[]{:S(2)}) collective-permute-start(bf16[152,512]{1,0:T(8,128)(2,1)} %rest_0_.1), channel_id=1, source_target_pairs={{0,16},{8,24},{16,0},{24,8},{32,48},{40,56},{48,32},{56,40},{64,80... | collective-permute-start | bytes 466952 | tf_op jit(solution)/shard_map/ppermute | solution.py:18
  10.9 96.9 %collective-permute-start.3 = (bf16[152,512]{1,0:T(8,128)(2,1)}, bf16[152,512]{1,0:T(8,128)(2,1)S(1)}, u32[]{:S(2)}, u32[]{:S(2)}) collective-permute-start(bf16[152,512]{1,0:T(8,128)(2,1)} %rest_0_.1), channel_id=1, source_target_pairs={{0,8},{8,0},{16,24},{24,16},{32,40},{40,32},{48,56},{56,48},{64,72... | collective-permute-start | bytes 466952 | tf_op jit(solution)/shard_map/ppermute | solution.py:18
  11.6 96.1 %collective-permute-start.2 = (bf16[152,512]{1,0:T(8,128)(2,1)}, bf16[152,512]{1,0:T(8,128)(2,1)S(1)}, u32[]{:S(2)}, u32[]{:S(2)}) collective-permute-start(bf16[152,512]{1,0:T(8,128)(2,1)} %rest_0_.1), channel_id=1, source_target_pairs={{0,4},{1,5},{2,6},{3,7},{4,0},{5,1},{6,2},{7,3},{8,12},{9,13},{10,... | collective-permute-start | bytes 466952 | tf_op jit(solution)/shard_map/ppermute | solution.py:18
  20.5 87.2 %collective-permute-start.1 = (bf16[152,512]{1,0:T(8,128)(2,1)}, bf16[152,512]{1,0:T(8,128)(2,1)S(1)}, u32[]{:S(2)}, u32[]{:S(2)}) collective-permute-start(bf16[152,512]{1,0:T(8,128)(2,1)} %rest_0_.1), channel_id=1, source_target_pairs={{0,2},{1,3},{2,0},{3,1},{4,6},{5,7},{6,4},{7,5},{8,10},{9,11},{10,... | collective-permute-start | bytes 466952 | tf_op jit(solution)/shard_map/ppermute | solution.py:18
  21.0 86.7 %collective-permute-start = (bf16[152,512]{1,0:T(8,128)(2,1)}, bf16[152,512]{1,0:T(8,128)(2,1)S(1)}, u32[]{:S(2)}, u32[]{:S(2)}) collective-permute-start(bf16[152,512]{1,0:T(8,128)(2,1)} %rest_0_.1), channel_id=1, source_target_pairs={{0,1},{1,0},{2,3},{3,2},{4,5},{5,4},{6,7},{7,6},{8,9},{9,8},{10,11... | collective-permute-start | bytes 466952 | tf_op jit(solution)/shard_map/ppermute | solution.py:18
  24.9 82.8 %collective-permute-start.7 = (bf16[152,512]{1,0:T(8,128)(2,1)}, bf16[152,512]{1,0:T(8,128)(2,1)S(1)}, u32[]{:S(2)}, u32[]{:S(2)}) collective-permute-start(bf16[152,512]{1,0:T(8,128)(2,1)} %rest_0_.1), channel_id=1, source_target_pairs={{0,128},{8,136},{16,144},{24,152},{32,160},{40,168},{48,176},{56,1... | collective-permute-start | bytes 466952 | tf_op jit(solution)/shard_map/ppermute | solution.py:18
  87.9 19.9 %copy-start = (bf16[8,152,152]{2,1,0:T(8,128)(2,1)S(1)}, bf16[8,152,152]{2,1,0:T(8,128)(2,1)}, u32[]{:S(2)}) copy-start(bf16[8,152,152]{2,1,0:T(8,128)(2,1)} %up_ref.3) | copy-start | bytes 1108996
  87.9 19.9 %copy-start.1 = (bf16[152,512]{1,0:T(8,128)(2,1)S(1)}, bf16[152,512]{1,0:T(8,128)(2,1)}, u32[]{:S(2)}) copy-start(bf16[152,512]{1,0:T(8,128)(2,1)} %rest_0_.1) | copy-start | bytes 466948

commit v2 on v1

v2 whole, which is shorter than its diff:
```python
import functools

import jax
import jax.numpy as jnp
from jax import lax
from jax.experimental import pallas as pl
from jax.experimental.pallas import tpu as pltpu
from jax.sharding import PartitionSpec as P

LEVELS = 3
LANES = 128
NT = (((1,), (1,)), ((), ()))


def from_partner(value, axis, stride):
    mask = 2**stride
    pairs = [(source, source ^ mask) for source in range(lax.axis_size(axis))]
    return lax.ppermute(value, axis, pairs)


def lift(rows, up_ref):
    surface = up_ref.shape[1]
    count = rows.shape[1] // 8
    total = None
    for octant in range(8):
        children = jnp.concatenate([rows[half, pl.ds(octant, count, stride=8), :] for half in range(2)], axis=1)
        children = children[:, :surface].astype(jnp.bfloat16)
        term = lax.dot_general(children, up_ref[octant], NT, preferred_element_type=jnp.float32)
        total = term if total is None else total + term
    return total


def upward_kernel(place_ref, fine_ref, up_ref, out_ref, *levels):
    surface, boxes = fine_ref.shape
    spot = lax.broadcasted_iota(jnp.int32, (boxes, boxes), 0) == lax.broadcasted_iota(jnp.int32, (boxes, boxes), 1)
    rows = lax.dot_general(
        spot.astype(jnp.float32).astype(jnp.bfloat16), fine_ref[...], NT, preferred_element_type=jnp.float32
    )
    for level in levels:
        level[0] = rows[:, :LANES]
        level[1, :, : surface - LANES] = rows[:, LANES:]
        rows = lift(level, up_ref).astype(jnp.bfloat16)
        rows = rows.astype(jnp.float32)
    octant = up_ref[place_ref[1]]
    term = lax.dot_general(rows.astype(jnp.bfloat16), octant, NT, preferred_element_type=jnp.float32)
    mine = lax.broadcasted_iota(jnp.int32, out_ref.shape, 0) == place_ref[0]
    out_ref[...] = jnp.where(mine, jnp.broadcast_to(term, out_ref.shape), 0.0)


def upward(place, coarse, fine_mult, up_operators):
    surface, boxes = fine_mult.shape
    vmem = pl.BlockSpec(memory_space=pltpu.VMEM)
    return pl.pallas_call(
        upward_kernel,
        in_specs=[pl.BlockSpec(memory_space=pltpu.SMEM), vmem, vmem],
        out_specs=vmem,
        out_shape=jax.ShapeDtypeStruct((coarse, surface), jnp.float32),
        scratch_shapes=[pltpu.VMEM((2, boxes // 8**level, LANES), jnp.float32) for level in range(LEVELS)],
        name="upward",
    )(place, fine_mult, up_operators)


PAIRS = 4
CHUNKS = 2


def translate_kernel(sections, idx_hbm, slots_ref, coarse_ref, far_ref, *rest):
    blocks = rest[:sections]
    fine_out, coarse_out, table, buf_a, buf_b, acc, *rest = rest[sections:]
    idx, sem = rest[:PAIRS], rest[PAIRS]
    bufs = (buf_a, buf_b)
    step = pl.program_id(0)
    last = pl.num_programs(0) - 1
    surface = far_ref.shape[1]
    boxes = blocks[0].shape[1]
    targets = acc.shape[0]
    tail = surface - LANES
    pairs = idx_hbm.shape[0] // 2

    def fetch(pair, slot):
        pair = jnp.minimum(pair, pairs - 1)
        return [
            pltpu.make_async_copy(idx_hbm.at[2 * pair + k], idx[slot].at[k], sem.at[slot, k]) for k in range(2)
        ]

    def start(pair, slot):
        for copy in fetch(pair, slot):
            copy.start()

    def wait(slot):
        for copy in fetch(0, slot):
            copy.wait()

    def put(first, rows):
        count = rows.shape[0]
        table[pl.ds(2 * first, count, stride=2), :] = rows[:, :LANES]
        table[pl.ds(2 * first + 1, count, stride=2), :] = jnp.concatenate(
            [rows[:, LANES:], jnp.zeros((count, LANES - tail), jnp.float32)], axis=1
        )

    def gather(where, buf, part=0, parts=1):
        size = targets // parts
        for k in range(2):
            for target in range(part * size, (part + 1) * size):
                buf[k, 2 * target : 2 * target + 2, :] = table[pl.ds(where[k, target], 2), :]

    def both(where, into, buf, pair):
        weights = []
        for k in range(2):
            weights += [far_ref[2 * pair + k], jnp.zeros((surface, LANES - tail), jnp.bfloat16)]
        weights = jnp.concatenate(weights, axis=1)
        size = targets // CHUNKS
        for part in range(CHUNKS):
            rows = []
            for k in range(2):
                rows += [buf[k, pl.ds(2 * part * size + half, size, stride=2), :] for half in range(2)]
            rows = jnp.concatenate([piece.astype(jnp.bfloat16) for piece in rows], axis=1)
            span = pl.ds(part * size, size)
            acc[span, :] += lax.dot_general(rows, weights, NT, preferred_element_type=jnp.float32)
            if where is not None:
                gather(where, into, part, CHUNKS)

    @pl.when(step == 0)
    def _():
        for slot in range(PAIRS):
            start(slot, slot)
        acc[...] = jnp.zeros_like(acc)
        number = lax.broadcasted_iota(jnp.int32, (boxes, boxes), 1)
        for section in range(sections):
            spot = (slots_ref[:, section : section + 1] == number).astype(jnp.float32).astype(jnp.bfloat16)
            put(
                section * boxes,
                lax.dot_general(spot, blocks[section][...], NT, preferred_element_type=jnp.float32),
            )
        put(sections * boxes, coarse_ref[...].astype(jnp.bfloat16).astype(jnp.float32))
        put(sections * boxes + coarse_ref.shape[0], jnp.zeros((8, surface), jnp.float32))
        wait(0)
        gather(idx[0], buf_a)
        start(PAIRS, 0)

    for pair in range(PAIRS - 1):
        slot = pair + 1
        wait(slot)

        @pl.when(step <= last)
        def _():
            both(idx[slot], bufs[slot % 2], bufs[pair % 2], pair)

        start(PAIRS * (step + 1) + slot, slot)

    @pl.when(step < last)
    def _():
        wait(0)

    @pl.when(step < last)
    def _():
        both(idx[0], bufs[0], bufs[1], PAIRS - 1)

    @pl.when(step < last)
    def _():
        start(PAIRS * (step + 2), 0)

    @pl.when(step == last)
    def _():
        both(None, None, bufs[1], PAIRS - 1)
        for slot in range(PAIRS):
            wait(slot)
        fine_out[...] = jnp.transpose(acc[:boxes, :])
        coarse_out[...] = acc[boxes:, :]


def translate(idx, slots, coarse, far_operators, blocks):
    offsets, targets = idx.shape
    surface, boxes = blocks[0].shape
    sections = len(blocks)
    rows = sections * boxes + coarse.shape[0] + 8
    whole = lambda *shape: pl.BlockSpec(shape, lambda step: (0,) * len(shape))
    return pl.pallas_call(
        functools.partial(translate_kernel, sections),
        grid=(offsets // (2 * PAIRS),),
        in_specs=[
            pl.BlockSpec(memory_space=pl.ANY),
            whole(*slots.shape),
            whole(*coarse.shape),
            pl.BlockSpec((2 * PAIRS, surface, surface), lambda step: (step, 0, 0)),
        ]
        + [whole(surface, boxes) for _ in blocks],
        out_specs=[whole(surface, boxes), whole(*coarse.shape)],
        out_shape=[
            jax.ShapeDtypeStruct((surface, boxes), jnp.float32),
            jax.ShapeDtypeStruct(coarse.shape, jnp.float32),
        ],
        scratch_shapes=[
            pltpu.VMEM((2 * rows, LANES), jnp.float32),
            pltpu.VMEM((2, 2 * targets, LANES), jnp.float32),
            pltpu.VMEM((2, 2 * targets, LANES), jnp.float32),
            pltpu.VMEM((targets, surface), jnp.float32),
        ]
        + [pltpu.SMEM((2, targets), jnp.int32) for _ in range(PAIRS)]
        + [pltpu.SemaphoreType.DMA((PAIRS, 2))],
        compiler_params=pltpu.CompilerParams(vmem_limit_bytes=48 << 20),
        name="translate",
    )(idx, slots, coarse, far_operators, *blocks)


def shards(fine_mult, up_operators, far_operators, far_list, ghost_list, coarse_list):
    surface, boxes = fine_mult.shape
    bits_y = lax.axis_size("hy").bit_length() - 1
    bits_x = lax.axis_size("hx").bit_length() - 1
    coarse_boxes = coarse_list.shape[1]
    bits = [("hy", bit) for bit in range(bits_y)] + [("hx", bit) for bit in range(bits_x)]
    order = bits[bits_y : bits_y + 3][::-1] + bits[bits_y + 3 :][::-1] + bits[:bits_y][::-1]
    ghosts = {bit: from_partner(fine_mult, *bit) for bit in order}
    blocks = [fine_mult] + [ghosts[bit] for bit in bits]
    sections = len(blocks)
    place = jnp.stack([lax.axis_index("hx"), lax.axis_index("hy")]).astype(jnp.int32)
    coarse = upward(place, coarse_boxes, fine_mult, up_operators)
    for bit in bits:
        coarse = coarse + from_partner(coarse, *bit)
    first_coarse = sections * boxes
    zero_row = first_coarse + coarse_boxes
    idx = jnp.concatenate(
        [
            2 * jnp.where(far_list < 0, zero_row, far_list),
            2 * jnp.where(coarse_list < 0, zero_row, coarse_list + first_coarse),
        ],
        axis=1,
    )
    slots = jnp.concatenate([jnp.arange(boxes, dtype=jnp.int32)[:, None], jnp.transpose(ghost_list[0])], axis=1)
    fine_check, coarse_check = translate(idx, slots, coarse, far_operators, blocks)
    return (fine_check, jnp.transpose(coarse_check))


def solution(mesh):
    placed = (
        P(None, ("hx", "hy")),
        P(),
        P(),
        P(None, ("hx", "hy")),
        P(("hx", "hy"), None, None),
        P(),
    )
    return jax.shard_map(
        shards, mesh=mesh, in_specs=placed, out_specs=(P(None, ("hx", "hy")), P()), check_vma=False
    )
```

time: 182 us -> 144 us (0.79)
  blocking collectives: 60.3 us -> 0 us
  waiting for transfers between devices: 1.59 us -> 15.2 us
  starting transfers between devices: 19.2 us -> 32.3 us
  Pallas kernels: 75.4 us -> 71.1 us
    all_gather x1 -> x0, blocking collectives: 60.3 us -> none  [shards(): poles = lax.all_gather(multipoles, ('hx', 'hy'), axis=0, tiled=True)]
    ppermute x8 -> x16, waiting for transfers between devices: 1.59 us -> 15.2 us  [from_partner(): return lax.ppermute(value, axis, pairs)]
    ppermute x8 -> x16, starting transfers between devices: 19.2 us -> 32.3 us  [from_partner(): return lax.ppermute(value, axis, pairs)]
    pallas_call x1, Pallas kernels: 72 us -> 67.5 us  [translate(): pl.pallas_call(functools.partial(translate_kernel, sections), grid=(offse...]
    unnamed x7 -> x4, local copies, waits for them, and re-layouts: 20.7 us -> 20.6 us
  transfers between devices with their start and end apart: 8 -> 16, of which waited for: 1 -> 7; matrix products, arithmetic and copies ran while one was open for 13% -> 16% of each run, Pallas kernels for 2% -> 0%
where the time goes in v2:
time: 144 us
  Pallas kernels  71.1 us (49%)
  starting transfers between devices  32.3 us (22%)
  local copies, waits for them, and re-layouts  20.8 us (14%)
  waiting for transfers between devices  15.2 us (11%)
  other arithmetic  3.13 us (2%)
    pallas_call x1, Pallas kernels, translate(): pl.pallas_call(functools.partial(translate_kernel, sections), grid=(offse...  67.5 us
    ppermute x16, starting transfers between devices, from_partner(): return lax.ppermute(value, axis, pairs)  32.3 us
    unnamed x4, local copies, waits for them, and re-layouts  20.6 us
    ppermute x16, waiting for transfers between devices, from_partner(): return lax.ppermute(value, axis, pairs)  15.2 us
    pallas_call x1, Pallas kernels, upward(): pl.pallas_call(upward_kernel, in_specs=[pl.BlockSpec(memory_space=pltpu.S...  3.59 us
  transfers between devices with their start and end apart: 16, of which 7 were waited for; matrix products, arithmetic and copies ran while one was open for 16% of the time, Pallas kernels for 0%

profile of v2, /device:TPU:1, one launch (start us, length us, event | category | flops | bytes accessed | tf_op | source)
XLA Modules:
  0.0 143.5 jit_solution(14114370462037049045)
XLA Ops:
  0.6 0.6 pad_add_fusion.2.place_ref
  1.2 3.6 %upward.1 = f32[32,152]{1,0:T(8,128)} custom-call(s32[2]{0:T(128)} %pad_add_fusion.2.place_ref, bf16[152,512]{1,0:T(8,128)(2,1)} %rest_0_.1, bf16[8,152,152]{2,1,0:T(8,128)(2,1)} %up_ref.1), custom_call_target="tpu_custom_call" | custom-call | tf_op jit(solution)/shard_map/upward/pallas_call | solution.py:53
  4.8 3.2 %collective-permute-start = (f32[32,152]{1,0:T(8,128)}, f32[32,152]{1,0:T(8,128)S(1)}, u32[]{:S(2)}, u32[]{:S(2)}) collective-permute-start(f32[32,152]{1,0:T(8,128)} %upward.1), channel_id=1, source_target_pairs={{0,1},{1,0},{2,3},{3,2},{4,5},{5,4},{6,7},{7,6},{8,9},{9,8},{10,11... | collective-permute-start | bytes 58376 | tf_op jit(solution)/shard_map/ppermute | solution.py:18
  8.0 1.1 collective-permute-done
  9.1 0.8 add.32
  9.8 0.0 collective-permute-start.1
  9.8 2.8 %collective-permute-done.1 = f32[32,152]{1,0:T(8,128)S(1)} collective-permute-done((f32[32,152]{1,0:T(8,128)S(1)}, f32[32,152]{1,0:T(8,128)S(1)}, u32[]{:S(2)}, u32[]{:S(2)}) %collective-permute-start.1) | collective-permute-done | bytes 19488 | tf_op jit(solution)/shard_map/ppermute | solution.py:18
  12.6 1.2 collective-permute-start.2
  13.8 3.1 %collective-permute-done.2 = f32[32,152]{1,0:T(8,128)S(1)} collective-permute-done((f32[32,152]{1,0:T(8,128)S(1)}, f32[32,152]{1,0:T(8,128)S(1)}, u32[]{:S(2)}, u32[]{:S(2)}) %collective-permute-start.2) | collective-permute-done | bytes 19488 | tf_op jit(solution)/shard_map/ppermute | solution.py:18
  16.9 0.0 collective-permute-start.3
  16.9 2.8 %collective-permute-done.3 = f32[32,152]{1,0:T(8,128)S(1)} collective-permute-done((f32[32,152]{1,0:T(8,128)S(1)}, f32[32,152]{1,0:T(8,128)S(1)}, u32[]{:S(2)}, u32[]{:S(2)}) %collective-permute-start.3) | collective-permute-done | bytes 19488 | tf_op jit(solution)/shard_map/ppermute | solution.py:18
  19.7 1.4 collective-permute-start.4
  21.1 2.2 %collective-permute-done.4 = f32[32,152]{1,0:T(8,128)S(1)} collective-permute-done((f32[32,152]{1,0:T(8,128)S(1)}, f32[32,152]{1,0:T(8,128)S(1)}, u32[]{:S(2)}, u32[]{:S(2)}) %collective-permute-start.4) | collective-permute-done | bytes 19488 | tf_op jit(solution)/shard_map/ppermute | solution.py:18
  23.3 5.2 %collective-permute-start.5 = (f32[32,152]{1,0:T(8,128)S(1)}, f32[32,152]{1,0:T(8,128)S(1)}, u32[]{:S(2)}, u32[]{:S(2)}) collective-permute-start(f32[32,152]{1,0:T(8,128)S(1)} %add.36), channel_id=1, source_target_pairs={{0,32},{8,40},{16,48},{24,56},{32,0},{40,8},{48,16},{56,24},{64,96... | collective-permute-start | bytes 58376 | tf_op jit(solution)/shard_map/ppermute | solution.py:18
  28.5 1.2 collective-permute-start.14
  29.7 0.1 collective-permute-start.13
  29.8 1.5 %collective-permute-start.12 = (bf16[152,512]{1,0:T(8,128)(2,1)}, bf16[152,512]{1,0:T(8,128)(2,1)S(1)}, u32[]{:S(2)}, u32[]{:S(2)}) collective-permute-start(bf16[152,512]{1,0:T(8,128)(2,1)} %rest_0_.1), channel_id=1, source_target_pairs={{0,16},{8,24},{16,0},{24,8},{32,48},{40,56},{48,32},{56,40},{64,80... | collective-permute-start | bytes 466952 | tf_op jit(solution)/shard_map/ppermute | solution.py:18
  31.4 1.5 %collective-permute-start.11 = (bf16[152,512]{1,0:T(8,128)(2,1)}, bf16[152,512]{1,0:T(8,128)(2,1)S(1)}, u32[]{:S(2)}, u32[]{:S(2)}) collective-permute-start(bf16[152,512]{1,0:T(8,128)(2,1)} %rest_0_.1), channel_id=1, source_target_pairs={{0,8},{8,0},{16,24},{24,16},{32,40},{40,32},{48,56},{56,48},{64,72... | collective-permute-start | bytes 466952 | tf_op jit(solution)/shard_map/ppermute | solution.py:18
  32.9 0.0 collective-permute-done.5
  32.9 0.3 collective-permute-start.6
  33.2 1.0 fusion
  34.3 0.9 copy.12
  35.1 0.9 collective-permute-done.6
  36.1 2.2 %collective-permute-start.7 = (f32[32,152]{1,0:T(8,128)S(1)}, f32[32,152]{1,0:T(8,128)S(1)}, u32[]{:S(2)}, u32[]{:S(2)}) collective-permute-start(f32[32,152]{1,0:T(8,128)S(1)} %add.38), channel_id=1, source_target_pairs={{0,128},{8,136},{16,144},{24,152},{32,160},{40,168},{48,176},{56,1... | collective-permute-start | bytes 58376 | tf_op jit(solution)/shard_map/ppermute | solution.py:18
  38.3 2.3 %collective-permute-done.7 = f32[32,152]{1,0:T(8,128)S(1)} collective-permute-done((f32[32,152]{1,0:T(8,128)S(1)}, f32[32,152]{1,0:T(8,128)S(1)}, u32[]{:S(2)}, u32[]{:S(2)}) %collective-permute-start.7) | collective-permute-done | bytes 19488 | tf_op jit(solution)/shard_map/ppermute | solution.py:18
  40.6 2.6 %collective-permute-start.10 = (bf16[152,512]{1,0:T(8,128)(2,1)}, bf16[152,512]{1,0:T(8,128)(2,1)S(1)}, u32[]{:S(2)}, u32[]{:S(2)}) collective-permute-start(bf16[152,512]{1,0:T(8,128)(2,1)} %rest_0_.1), channel_id=1, source_target_pairs={{0,4},{1,5},{2,6},{3,7},{4,0},{5,1},{6,2},{7,3},{8,12},{9,13},{10,... | collective-permute-start | bytes 466952 | tf_op jit(solution)/shard_map/ppermute | solution.py:18
  43.2 0.0 collective-permute-done.14.rest_7_
  43.2 0.4 collective-permute-start.9
  43.6 0.0 collective-permute-done.13.rest_6_
  43.6 9.0 %collective-permute-start.8 = (bf16[152,512]{1,0:T(8,128)(2,1)}, bf16[152,512]{1,0:T(8,128)(2,1)S(1)}, u32[]{:S(2)}, u32[]{:S(2)}) collective-permute-start(bf16[152,512]{1,0:T(8,128)(2,1)} %rest_0_.1), channel_id=1, source_target_pairs={{0,1},{1,0},{2,3},{3,2},{4,5},{5,4},{6,7},{7,6},{8,9},{9,8},{10,11... | collective-permute-start | bytes 466952 | tf_op jit(solution)/shard_map/ppermute | solution.py:18
  52.6 0.0 collective-permute-done.12.rest_5_
  52.6 2.5 %collective-permute-start.15 = (bf16[152,512]{1,0:T(8,128)(2,1)}, bf16[152,512]{1,0:T(8,128)(2,1)S(1)}, u32[]{:S(2)}, u32[]{:S(2)}) collective-permute-start(bf16[152,512]{1,0:T(8,128)(2,1)} %rest_0_.1), channel_id=1, source_target_pairs={{0,128},{8,136},{16,144},{24,152},{32,160},{40,168},{48,176},{56,1... | collective-permute-start | bytes 466952 | tf_op jit(solution)/shard_map/ppermute | solution.py:18
  55.0 0.7 pad_add_fusion.1
  55.8 0.1 copy.14.slots_ref
  55.9 0.0 copy-start
  55.9 19.8 %copy.15.far_ref = bf16[160,152,152]{2,1,0:T(8,128)(2,1)} copy(bf16[160,152,152]{0,2,1:T(8,128)(2,1)} %param.8) | data formatting | bytes 14786560 | tf_op args[2]
  75.7 0.0 collective-permute-done.11.rest_4_
  75.8 0.0 collective-permute-done.10.rest_3_
  75.8 0.0 collective-permute-done.9.rest_2_
  75.8 0.0 collective-permute-done.8.rest_1_
  75.8 0.0 collective-permute-done.15.rest_8_
  75.8 0.0 copy-done
  75.8 67.5 %translate.1 = (f32[152,512]{1,0:T(8,128)}, f32[32,152]{1,0:T(8,128)}) custom-call(s32[160,544]{1,0:T(8,128)S(1)} %pad_add_fusion.idx_hbm, s32[512,9]{1,0:T(8,128)S(1)} %copy.14.slots_ref, f32[32,152]{1,0:T(8,128)S(1)} %add.39.coarse_ref, bf16[160,152,152]{2,1,0:T(8,128)(2,1)} %copy.15.far_ref, bf16[152,512]{1,0:T(8,128)(2,1)S(1)} %copy-done, ...), custom_call_target="tpu_custom_call" | custom-call | tf_op jit(solution)/shard_map/translate/pallas_call | solution.py:178
  (10 shorter events, 0.1 us)
Async XLA Ops:
  4.8 4.3 %collective-permute-start = (f32[32,152]{1,0:T(8,128)}, f32[32,152]{1,0:T(8,128)S(1)}, u32[]{:S(2)}, u32[]{:S(2)}) collective-permute-start(f32[32,152]{1,0:T(8,128)} %upward.1), channel_id=1, source_target_pairs={{0,1},{1,0},{2,3},{3,2},{4,5},{5,4},{6,7},{7,6},{8,9},{9,8},{10,11... | collective-permute-start | bytes 58376 | tf_op jit(solution)/shard_map/ppermute | solution.py:18
  9.8 2.8 %collective-permute-start.1 = (f32[32,152]{1,0:T(8,128)S(1)}, f32[32,152]{1,0:T(8,128)S(1)}, u32[]{:S(2)}, u32[]{:S(2)}) collective-permute-start(f32[32,152]{1,0:T(8,128)S(1)} %add.32), channel_id=1, source_target_pairs={{0,2},{1,3},{2,0},{3,1},{4,6},{5,7},{6,4},{7,5},{8,10},{9,11},{10,... | collective-permute-start | bytes 58376 | tf_op jit(solution)/shard_map/ppermute | solution.py:18
  12.6 4.3 %collective-permute-start.2 = (f32[32,152]{1,0:T(8,128)S(1)}, f32[32,152]{1,0:T(8,128)S(1)}, u32[]{:S(2)}, u32[]{:S(2)}) collective-permute-start(f32[32,152]{1,0:T(8,128)S(1)} %add.33), channel_id=1, source_target_pairs={{0,4},{1,5},{2,6},{3,7},{4,0},{5,1},{6,2},{7,3},{8,12},{9,13},{10,... | collective-permute-start | bytes 58376 | tf_op jit(solution)/shard_map/ppermute | solution.py:18
  16.9 2.8 %collective-permute-start.3 = (f32[32,152]{1,0:T(8,128)S(1)}, f32[32,152]{1,0:T(8,128)S(1)}, u32[]{:S(2)}, u32[]{:S(2)}) collective-permute-start(f32[32,152]{1,0:T(8,128)S(1)} %add.34), channel_id=1, source_target_pairs={{0,8},{8,0},{16,24},{24,16},{32,40},{40,32},{48,56},{56,48},{64,72... | collective-permute-start | bytes 58376 | tf_op jit(solution)/shard_map/ppermute | solution.py:18
  19.7 3.7 %collective-permute-start.4 = (f32[32,152]{1,0:T(8,128)S(1)}, f32[32,152]{1,0:T(8,128)S(1)}, u32[]{:S(2)}, u32[]{:S(2)}) collective-permute-start(f32[32,152]{1,0:T(8,128)S(1)} %add.35), channel_id=1, source_target_pairs={{0,16},{8,24},{16,0},{24,8},{32,48},{40,56},{48,32},{56,40},{64,80... | collective-permute-start | bytes 58376 | tf_op jit(solution)/shard_map/ppermute | solution.py:18
  23.3 9.5 %collective-permute-start.5 = (f32[32,152]{1,0:T(8,128)S(1)}, f32[32,152]{1,0:T(8,128)S(1)}, u32[]{:S(2)}, u32[]{:S(2)}) collective-permute-start(f32[32,152]{1,0:T(8,128)S(1)} %add.36), channel_id=1, source_target_pairs={{0,32},{8,40},{16,48},{24,56},{32,0},{40,8},{48,16},{56,24},{64,96... | collective-permute-start | bytes 58376 | tf_op jit(solution)/shard_map/ppermute | solution.py:18
  28.5 14.7 %collective-permute-start.14 = (bf16[152,512]{1,0:T(8,128)(2,1)}, bf16[152,512]{1,0:T(8,128)(2,1)S(1)}, u32[]{:S(2)}, u32[]{:S(2)}) collective-permute-start(bf16[152,512]{1,0:T(8,128)(2,1)} %rest_0_.1), channel_id=1, source_target_pairs={{0,64},{8,72},{16,80},{24,88},{32,96},{40,104},{48,112},{56,120},{... | collective-permute-start | bytes 466952 | tf_op jit(solution)/shard_map/ppermute | solution.py:18
  29.7 13.9 %collective-permute-start.13 = (bf16[152,512]{1,0:T(8,128)(2,1)}, bf16[152,512]{1,0:T(8,128)(2,1)S(1)}, u32[]{:S(2)}, u32[]{:S(2)}) collective-permute-start(bf16[152,512]{1,0:T(8,128)(2,1)} %rest_0_.1), channel_id=1, source_target_pairs={{0,32},{8,40},{16,48},{24,56},{32,0},{40,8},{48,16},{56,24},{64,96... | collective-permute-start | bytes 466952 | tf_op jit(solution)/shard_map/ppermute | solution.py:18
  29.8 22.7 %collective-permute-start.12 = (bf16[152,512]{1,0:T(8,128)(2,1)}, bf16[152,512]{1,0:T(8,128)(2,1)S(1)}, u32[]{:S(2)}, u32[]{:S(2)}) collective-permute-start(bf16[152,512]{1,0:T(8,128)(2,1)} %rest_0_.1), channel_id=1, source_target_pairs={{0,16},{8,24},{16,0},{24,8},{32,48},{40,56},{48,32},{56,40},{64,80... | collective-permute-start | bytes 466952 | tf_op jit(solution)/shard_map/ppermute | solution.py:18
  31.4 44.4 %collective-permute-start.11 = (bf16[152,512]{1,0:T(8,128)(2,1)}, bf16[152,512]{1,0:T(8,128)(2,1)S(1)}, u32[]{:S(2)}, u32[]{:S(2)}) collective-permute-start(bf16[152,512]{1,0:T(8,128)(2,1)} %rest_0_.1), channel_id=1, source_target_pairs={{0,8},{8,0},{16,24},{24,16},{32,40},{40,32},{48,56},{56,48},{64,72... | collective-permute-start | bytes 466952 | tf_op jit(solution)/shard_map/ppermute | solution.py:18
  32.9 3.1 %collective-permute-start.6 = (f32[32,152]{1,0:T(8,128)S(1)}, f32[32,152]{1,0:T(8,128)S(1)}, u32[]{:S(2)}, u32[]{:S(2)}) collective-permute-start(f32[32,152]{1,0:T(8,128)S(1)} %add.37), channel_id=1, source_target_pairs={{0,64},{8,72},{16,80},{24,88},{32,96},{40,104},{48,112},{56,120},{... | collective-permute-start | bytes 58376 | tf_op jit(solution)/shard_map/ppermute | solution.py:18
  36.1 4.6 %collective-permute-start.7 = (f32[32,152]{1,0:T(8,128)S(1)}, f32[32,152]{1,0:T(8,128)S(1)}, u32[]{:S(2)}, u32[]{:S(2)}) collective-permute-start(f32[32,152]{1,0:T(8,128)S(1)} %add.38), channel_id=1, source_target_pairs={{0,128},{8,136},{16,144},{24,152},{32,160},{40,168},{48,176},{56,1... | collective-permute-start | bytes 58376 | tf_op jit(solution)/shard_map/ppermute | solution.py:18
  40.6 35.1 %collective-permute-start.10 = (bf16[152,512]{1,0:T(8,128)(2,1)}, bf16[152,512]{1,0:T(8,128)(2,1)S(1)}, u32[]{:S(2)}, u32[]{:S(2)}) collective-permute-start(bf16[152,512]{1,0:T(8,128)(2,1)} %rest_0_.1), channel_id=1, source_target_pairs={{0,4},{1,5},{2,6},{3,7},{4,0},{5,1},{6,2},{7,3},{8,12},{9,13},{10,... | collective-permute-start | bytes 466952 | tf_op jit(solution)/shard_map/ppermute | solution.py:18
  43.2 32.6 %collective-permute-start.9 = (bf16[152,512]{1,0:T(8,128)(2,1)}, bf16[152,512]{1,0:T(8,128)(2,1)S(1)}, u32[]{:S(2)}, u32[]{:S(2)}) collective-permute-start(bf16[152,512]{1,0:T(8,128)(2,1)} %rest_0_.1), channel_id=1, source_target_pairs={{0,2},{1,3},{2,0},{3,1},{4,6},{5,7},{6,4},{7,5},{8,10},{9,11},{10,... | collective-permute-start | bytes 466952 | tf_op jit(solution)/shard_map/ppermute | solution.py:18
  43.6 32.2 %collective-permute-start.8 = (bf16[152,512]{1,0:T(8,128)(2,1)}, bf16[152,512]{1,0:T(8,128)(2,1)S(1)}, u32[]{:S(2)}, u32[]{:S(2)}) collective-permute-start(bf16[152,512]{1,0:T(8,128)(2,1)} %rest_0_.1), channel_id=1, source_target_pairs={{0,1},{1,0},{2,3},{3,2},{4,5},{5,4},{6,7},{7,6},{8,9},{9,8},{10,11... | collective-permute-start | bytes 466952 | tf_op jit(solution)/shard_map/ppermute | solution.py:18
  52.6 23.2 %collective-permute-start.15 = (bf16[152,512]{1,0:T(8,128)(2,1)}, bf16[152,512]{1,0:T(8,128)(2,1)S(1)}, u32[]{:S(2)}, u32[]{:S(2)}) collective-permute-start(bf16[152,512]{1,0:T(8,128)(2,1)} %rest_0_.1), channel_id=1, source_target_pairs={{0,128},{8,136},{16,144},{24,152},{32,160},{40,168},{48,176},{56,1... | collective-permute-start | bytes 466952 | tf_op jit(solution)/shard_map/ppermute | solution.py:18
  55.9 19.9 %copy-start = (bf16[152,512]{1,0:T(8,128)(2,1)S(1)}, bf16[152,512]{1,0:T(8,128)(2,1)}, u32[]{:S(2)}) copy-start(bf16[152,512]{1,0:T(8,128)(2,1)} %rest_0_.1) | copy-start | bytes 466948

commit v3 on v2

--- a/solution.py
+++ b/solution.py
@@ -60,27 +60,84 @@
     )(place, fine_mult, up_operators)
 
 
-PAIRS = 4
+STRIP = 16
+PIECE = 32
+GROUP = 2
+PHASES = 8
 CHUNKS = 2
 
 
-def translate_kernel(sections, idx_hbm, slots_ref, coarse_ref, far_ref, *rest):
+def relayout_kernel(far_ref, out_ref, low, high):
+    rows, surface, offsets = far_ref.shape
+    pitch = low.shape[0] // offsets
+    spot = lax.broadcasted_iota(jnp.int32, (offsets, offsets), 0) == lax.broadcasted_iota(
+        jnp.int32, (offsets, offsets), 1
+    )
+    spot = spot.astype(jnp.float32).astype(jnp.bfloat16)
+    gap = jnp.zeros((offsets, 2 * LANES - surface), jnp.float32)
+    for row in range(rows):
+        turned = lax.dot_general(spot, far_ref[row], NT, preferred_element_type=jnp.float32)
+        low[pl.ds(row, offsets, stride=pitch), :] = turned[:, :LANES]
+        high[pl.ds(row, offsets, stride=pitch), :] = jnp.concatenate([turned[:, LANES:], gap], axis=1)
+    for offset in range(offsets):
+        span = pl.ds(offset * pitch, rows)
+        out_ref[offset, :, :LANES] = low[span, :].astype(jnp.bfloat16)
+        out_ref[offset, :, LANES:] = high[span, :][:, : surface - LANES].astype(jnp.bfloat16)
+
+
+def relayout(far_turned, piece):
+    surface, _, offsets = far_turned.shape
+    count = min(PIECE, surface - piece * PIECE)
+    first = piece * PIECE // STRIP
+    return pl.pallas_call(
+        relayout_kernel,
+        grid=(-(-count // STRIP),),
+        in_specs=[pl.BlockSpec((STRIP, surface, offsets), lambda step: (first + step, 0, 0))],
+        out_specs=pl.BlockSpec((offsets, STRIP, surface), lambda step: (0, step, 0)),
+        out_shape=jax.ShapeDtypeStruct((offsets, count, surface), jnp.bfloat16),
+        scratch_shapes=[pltpu.VMEM((offsets * (STRIP + 1), LANES), jnp.float32) for _ in range(2)],
+        compiler_params=pltpu.CompilerParams(vmem_limit_bytes=16 << 20),
+        cost_estimate=pl.CostEstimate(
+            flops=2 * offsets * offsets * count * surface, bytes_accessed=6 * offsets * count * surface, transcendentals=0
+        ),
+        name="relayout",
+    )(far_turned)
+
+
+def add_kernel(a_ref, b_ref, *rest):
+    rest[-1][...] = a_ref[...] + b_ref[...]
+
+
+def add_after(a, b, others):
+    vmem = pl.BlockSpec(memory_space=pltpu.VMEM)
+    return pl.pallas_call(
+        add_kernel,
+        in_specs=[vmem, vmem] + [pl.BlockSpec(memory_space=pl.ANY) for _ in others],
+        out_specs=vmem,
+        out_shape=jax.ShapeDtypeStruct(a.shape, a.dtype),
+        cost_estimate=pl.CostEstimate(flops=a.size, bytes_accessed=12 * a.size, transcendentals=0),
+        name="add",
+    )(a, b, *others)
+
+
+def translate_kernel(sections, pieces, idx_hbm, slots_ref, coarse_ref, *rest):
+    far_refs, rest = rest[:pieces], rest[pieces:]
     blocks = rest[:sections]
     fine_out, coarse_out, table, buf_a, buf_b, acc, *rest = rest[sections:]
-    idx, sem = rest[:PAIRS], rest[PAIRS]
+    idx, sem = rest[:PHASES], rest[PHASES]
     bufs = (buf_a, buf_b)
     step = pl.program_id(0)
     last = pl.num_programs(0) - 1
-    surface = far_ref.shape[1]
+    surface = far_refs[0].shape[2]
     boxes = blocks[0].shape[1]
     targets = acc.shape[0]
     tail = surface - LANES
-    pairs = idx_hbm.shape[0] // 2
+    groups = idx_hbm.shape[0] // GROUP
 
     def fetch(pair, slot):
-        pair = jnp.minimum(pair, pairs - 1)
+        pair = jnp.minimum(pair, groups - 1)
         return [
-            pltpu.make_async_copy(idx_hbm.at[2 * pair + k], idx[slot].at[k], sem.at[slot, k]) for k in range(2)
+            pltpu.make_async_copy(idx_hbm.at[GROUP * pair + k], idx[slot].at[k], sem.at[slot, k]) for k in range(GROUP)
         ]
 
     def start(pair, slot):
@@ -100,19 +157,20 @@
 
     def gather(where, buf, part=0, parts=1):
         size = targets // parts
-        for k in range(2):
+        for k in range(GROUP):
             for target in range(part * size, (part + 1) * size):
                 buf[k, 2 * target : 2 * target + 2, :] = table[pl.ds(where[k, target], 2), :]
 
     def both(where, into, buf, pair):
         weights = []
-        for k in range(2):
-            weights += [far_ref[2 * pair + k], jnp.zeros((surface, LANES - tail), jnp.bfloat16)]
+        for k in range(GROUP):
+            operator = jnp.concatenate([far_ref[GROUP * pair + k] for far_ref in far_refs], axis=0)
+            weights += [operator, jnp.zeros((surface, LANES - tail), jnp.bfloat16)]
         weights = jnp.concatenate(weights, axis=1)
         size = targets // CHUNKS
         for part in range(CHUNKS):
             rows = []
-            for k in range(2):
+            for k in range(GROUP):
                 rows += [buf[k, pl.ds(2 * part * size + half, size, stride=2), :] for half in range(2)]
             rows = jnp.concatenate([piece.astype(jnp.bfloat16) for piece in rows], axis=1)
             span = pl.ds(part * size, size)
@@ -122,7 +180,7 @@
 
     @pl.when(step == 0)
     def _():
-        for slot in range(PAIRS):
+        for slot in range(PHASES):
             start(slot, slot)
         acc[...] = jnp.zeros_like(acc)
         number = lax.broadcasted_iota(jnp.int32, (boxes, boxes), 1)
@@ -136,9 +194,9 @@
         put(sections * boxes + coarse_ref.shape[0], jnp.zeros((8, surface), jnp.float32))
         wait(0)
         gather(idx[0], buf_a)
-        start(PAIRS, 0)
-
-    for pair in range(PAIRS - 1):
+        start(PHASES, 0)
+
+    for pair in range(PHASES - 1):
         slot = pair + 1
         wait(slot)
 
@@ -146,7 +204,7 @@
         def _():
             both(idx[slot], bufs[slot % 2], bufs[pair % 2], pair)
 
-        start(PAIRS * (step + 1) + slot, slot)
+        start(PHASES * (step + 1) + slot, slot)
 
     @pl.when(step < last)
     def _():
@@ -154,36 +212,36 @@
 
     @pl.when(step < last)
     def _():
-        both(idx[0], bufs[0], bufs[1], PAIRS - 1)
+        both(idx[0], bufs[0], bufs[1], PHASES - 1)
 
     @pl.when(step < last)
     def _():
-        start(PAIRS * (step + 2), 0)
+        start(PHASES * (step + 2), 0)
 
     @pl.when(step == last)
     def _():
-        both(None, None, bufs[1], PAIRS - 1)
-        for slot in range(PAIRS):
+        both(None, None, bufs[1], PHASES - 1)
+        for slot in range(PHASES):
             wait(slot)
         fine_out[...] = jnp.transpose(acc[:boxes, :])
         coarse_out[...] = acc[boxes:, :]
 
 
-def translate(idx, slots, coarse, far_operators, blocks):
+def translate(idx, slots, coarse, far_pieces, blocks):
     offsets, targets = idx.shape
     surface, boxes = blocks[0].shape
     sections = len(blocks)
     rows = sections * boxes + coarse.shape[0] + 8
     whole = lambda *shape: pl.BlockSpec(shape, lambda step: (0,) * len(shape))
     return pl.pallas_call(
-        functools.partial(translate_kernel, sections),
-        grid=(offsets // (2 * PAIRS),),
+        functools.partial(translate_kernel, sections, len(far_pieces)),
+        grid=(offsets // (GROUP * PHASES),),
         in_specs=[
             pl.BlockSpec(memory_space=pl.ANY),
             whole(*slots.shape),
             whole(*coarse.shape),
-            pl.BlockSpec((2 * PAIRS, surface, surface), lambda step: (step, 0, 0)),
         ]
+        + [pl.BlockSpec((GROUP * PHASES, *piece.shape[1:]), lambda step: (step, 0, 0)) for piece in far_pieces]
         + [whole(surface, boxes) for _ in blocks],
         out_specs=[whole(surface, boxes), whole(*coarse.shape)],
         out_shape=[
@@ -192,15 +250,15 @@
         ],
         scratch_shapes=[
             pltpu.VMEM((2 * rows, LANES), jnp.float32),
-            pltpu.VMEM((2, 2 * targets, LANES), jnp.float32),
-            pltpu.VMEM((2, 2 * targets, LANES), jnp.float32),
+            pltpu.VMEM((GROUP, 2 * targets, LANES), jnp.float32),
+            pltpu.VMEM((GROUP, 2 * targets, LANES), jnp.float32),
             pltpu.VMEM((targets, surface), jnp.float32),
         ]
-        + [pltpu.SMEM((2, targets), jnp.int32) for _ in range(PAIRS)]
-        + [pltpu.SemaphoreType.DMA((PAIRS, 2))],
+        + [pltpu.SMEM((GROUP, targets), jnp.int32) for _ in range(PHASES)]
+        + [pltpu.SemaphoreType.DMA((PHASES, GROUP))],
         compiler_params=pltpu.CompilerParams(vmem_limit_bytes=48 << 20),
         name="translate",
-    )(idx, slots, coarse, far_operators, *blocks)
+    )(idx, slots, coarse, *far_pieces, *blocks)
 
 
 def shards(fine_mult, up_operators, far_operators, far_list, ghost_list, coarse_list):
@@ -215,8 +273,13 @@
     sections = len(blocks)
     place = jnp.stack([lax.axis_index("hx"), lax.axis_index("hy")]).astype(jnp.int32)
     coarse = upward(place, coarse_boxes, fine_mult, up_operators)
-    for bit in bits:
-        coarse = coarse + from_partner(coarse, *bit)
+    far_turned = jnp.transpose(far_operators, (1, 2, 0))
+    pieces = [relayout(far_turned, piece) for piece in range(-(-surface // PIECE))]
+    due = [[piece] for piece in pieces] + [[] for _ in range(len(bits) - len(pieces))]
+    for number, bit in enumerate(order):
+        due[min(4 + number // 2, len(bits) - 1)].append(ghosts[bit])
+    for bit, others in zip(bits, due):
+        coarse = add_after(coarse, from_partner(coarse, *bit), others)
     first_coarse = sections * boxes
     zero_row = first_coarse + coarse_boxes
     idx = jnp.concatenate(
@@ -227,7 +290,7 @@
         axis=1,
     )
     slots = jnp.concatenate([jnp.arange(boxes, dtype=jnp.int32)[:, None], jnp.transpose(ghost_list[0])], axis=1)
-    fine_check, coarse_check = translate(idx, slots, coarse, far_operators, blocks)
+    fine_check, coarse_check = translate(idx, slots, coarse, pieces, blocks)
     return (fine_check, jnp.transpose(coarse_check))
 
 

time: 144 us -> 168 us (1.17)
  the two profiles are of different devices: /device:TPU:1 before, /device:TPU:24 now
where the time goes in v3:
time: 168 us; the launch traced here: 167 us
  Pallas kernels  86.9 us (52%)
  local copies, waits for them, and re-layouts  38.8 us (23%)
  starting transfers between devices  22.5 us (13%)
  waiting for transfers between devices  15.1 us (9%)
  other arithmetic  2.25 us (1%)
    pallas_call x1, Pallas kernels, translate(): pl.pallas_call(functools.partial(translate_kernel, sections, len(far_piec...  64.8 us
    unnamed x73, local copies, waits for them, and re-layouts  38.7 us
    ppermute x16, starting transfers between devices, from_partner(): return lax.ppermute(value, axis, pairs)  22.5 us
    ppermute x16, waiting for transfers between devices, from_partner(): return lax.ppermute(value, axis, pairs)  15.1 us
    pallas_call x8, Pallas kernels, add_after(): pl.pallas_call(add_kernel, in_specs=[vmem, vmem] + [pl.BlockSpec(memory_s...  11.1 us
    pallas_call x5, Pallas kernels, relayout(): pl.pallas_call(relayout_kernel, grid=(-(-count // STRIP),), in_specs=[pl....  7.42 us
    pallas_call x1, Pallas kernels, upward(): pl.pallas_call(upward_kernel, in_specs=[pl.BlockSpec(memory_space=pltpu.S...  3.58 us
  transfers between devices with their start and end apart: 16, of which 5 were waited for; matrix products, arithmetic and copies ran while one was open for 1% of the time, Pallas kernels for 12%

profile of v3, /device:TPU:24, one launch (start us, length us, event | category | flops | bytes accessed | tf_op | source)
XLA Modules:
  0.0 166.6 jit_solution(17558711186320125260)
XLA Ops:
  0.6 1.3 collective-permute-start.12
  2.0 1.5 collective-permute-start.11
  3.4 3.3 %collective-permute-start.6 = (bf16[152,512]{1,0:T(8,128)(2,1)}, bf16[152,512]{1,0:T(8,128)(2,1)S(1)}, u32[]{:S(2)}, u32[]{:S(2)}) collective-permute-start(bf16[152,512]{1,0:T(8,128)(2,1)} %rest_5_.1), channel_id=1, source_target_pairs={{0,16},{8,24},{16,0},{24,8},{32,48},{40,56},{48,32},{56,40},{64,80... | collective-permute-start | bytes 466952 | tf_op jit(solution)/shard_map/ppermute | solution.py:18
  6.7 5.4 %collective-permute-start.5 = (bf16[152,512]{1,0:T(8,128)(2,1)}, bf16[152,512]{1,0:T(8,128)(2,1)S(1)}, u32[]{:S(2)}, u32[]{:S(2)}) collective-permute-start(bf16[152,512]{1,0:T(8,128)(2,1)} %rest_5_.1), channel_id=1, source_target_pairs={{0,32},{8,40},{16,48},{24,56},{32,0},{40,8},{48,16},{56,24},{64,96... | collective-permute-start | bytes 466952 | tf_op jit(solution)/shard_map/ppermute | solution.py:18
  12.1 0.6 pad_add_fusion.2.place_ref
  12.7 3.6 %upward.1.a_ref = f32[32,152]{1,0:T(8,128)} custom-call(s32[2]{0:T(128)} %pad_add_fusion.2.place_ref, bf16[152,512]{1,0:T(8,128)(2,1)} %rest_5_.1, bf16[8,152,152]{2,1,0:T(8,128)(2,1)} %up_ref.1), custom_call_target="tpu_custom_call" | custom-call | tf_op jit(solution)/shard_map/upward/pallas_call | solution.py:53
  16.3 0.0 collective-permute-start
  16.3 4.4 %copy-done = bf16[160,152,152]{0,2,1:T(8,128)(2,1)S(1)} copy-done((bf16[160,152,152]{0,2,1:T(8,128)(2,1)S(1)}, bf16[160,152,152]{0,2,1:T(8,128)(2,1)}, u32[]{:S(2)}) %copy-start) | copy-done | bytes 7393304
  20.7 1.5 relayout.5.rest_0_
  22.2 1.5 copy-done.5
  23.7 0.6 copy-done.27
  24.3 1.4 add.24.a_ref
  25.7 4.4 %copy-done.1 = bf16[160,152,152]{0,2,1:T(8,128)(2,1)S(1)} copy-done((bf16[160,152,152]{0,2,1:T(8,128)(2,1)S(1)}, bf16[160,152,152]{0,2,1:T(8,128)(2,1)}, u32[]{:S(2)}) %copy-start.1) | copy-done | bytes 7393304
  30.1 1.5 relayout.6.rest_0_.rest_1_
  31.6 1.5 copy-done.6
  33.1 0.6 copy-done.28
  33.7 1.4 add.25.a_ref
  35.1 3.6 %collective-permute-start.2 = (f32[32,152]{1,0:T(8,128)}, f32[32,152]{1,0:T(8,128)S(1)}, u32[]{:S(2)}, u32[]{:S(2)}) collective-permute-start(f32[32,152]{1,0:T(8,128)} %add.25.a_ref), channel_id=1, source_target_pairs={{0,4},{1,5},{2,6},{3,7},{4,0},{5,1},{6,2},{7,3},{8,12},{9,13},{10,... | collective-permute-start | bytes 58376 | tf_op jit(solution)/shard_map/ppermute | solution.py:18
  38.8 4.4 %copy-done.2 = bf16[160,152,152]{0,2,1:T(8,128)(2,1)S(1)} copy-done((bf16[160,152,152]{0,2,1:T(8,128)(2,1)S(1)}, bf16[160,152,152]{0,2,1:T(8,128)(2,1)}, u32[]{:S(2)}) %copy-start.2) | copy-done | bytes 7393304
  43.1 1.5 relayout.7.rest_0_.rest_2_
  44.6 1.5 copy-done.7
  46.1 0.6 copy-done.29
  46.8 1.4 add.26.a_ref
  48.1 1.0 collective-permute-start.3
  49.2 4.4 %copy-done.3 = bf16[160,152,152]{0,2,1:T(8,128)(2,1)S(1)} copy-done((bf16[160,152,152]{0,2,1:T(8,128)(2,1)S(1)}, bf16[160,152,152]{0,2,1:T(8,128)(2,1)}, u32[]{:S(2)}) %copy-start.3) | copy-done | bytes 7393304
  53.5 1.5 relayout.8.rest_0_.rest_3_
  55.0 1.6 copy-done.8
  56.6 0.6 copy-done.30
  57.2 1.4 add.27.a_ref
  58.6 1.5 collective-permute-start.4
  60.1 0.1 copy.11
  60.2 4.4 %copy-done.4 = bf16[160,152,152]{0,2,1:T(8,128)(2,1)S(1)} copy-done((bf16[160,152,152]{0,2,1:T(8,128)(2,1)S(1)}, bf16[160,152,152]{0,2,1:T(8,128)(2,1)}, u32[]{:S(2)}) %copy-start.4) | copy-done | bytes 7393304
  64.6 1.4 relayout.9.rest_0_.rest_4_
  66.0 1.3 copy-done.9
  67.4 2.8 %collective-permute-start.9 = (bf16[152,512]{1,0:T(8,128)(2,1)S(1)}, bf16[152,512]{1,0:T(8,128)(2,1)S(1)}, u32[]{:S(2)}, u32[]{:S(2)}) collective-permute-start(bf16[152,512]{1,0:T(8,128)(2,1)S(1)} %copy-done.15), channel_id=1, source_target_pairs={{0,128},{8,136},{16,144},{24,152},{32,160},{40,168},{48,176},{56,1... | collective-permute-start | bytes 466952 | tf_op jit(solution)/shard_map/ppermute | solution.py:18
  70.2 1.0 collective-permute-start.8
  71.2 0.0 copy-start.13
  71.2 0.7 copy-done.13
  71.9 1.4 add.28.a_ref
  73.3 0.0 collective-permute-start.7
  73.3 0.7 select_multiply_fusion
  73.9 0.4 collective-permute-done.9.rest_1_.rest_13_
  74.3 0.1 collective-permute-start.14
  74.4 1.4 collective-permute-done.8.rest_0_.rest_9_
  75.8 0.0 collective-permute-start.15
  75.8 5.7 %collective-permute-done.7.b_ref = f32[32,152]{1,0:T(8,128)S(1)} collective-permute-done((f32[32,152]{1,0:T(8,128)}, f32[32,152]{1,0:T(8,128)S(1)}, u32[]{:S(2)}, u32[]{:S(2)}) %collective-permute-start.7) | collective-permute-done | bytes 19488 | tf_op jit(solution)/shard_map/ppermute | solution.py:18
  81.5 0.6 copy-done.32
  82.1 1.4 add.29.a_ref
  83.5 0.2 collective-permute-start.10
  83.7 0.9 pad_add_fusion.idx_hbm
  84.7 2.9 %collective-permute-done.10.b_ref = f32[32,152]{1,0:T(8,128)S(1)} collective-permute-done((f32[32,152]{1,0:T(8,128)}, f32[32,152]{1,0:T(8,128)S(1)}, u32[]{:S(2)}, u32[]{:S(2)}) %collective-permute-start.10) | collective-permute-done | bytes 19488 | tf_op jit(solution)/shard_map/ppermute | solution.py:18
  87.6 0.6 copy-done.34
  88.2 1.4 add.30.a_ref
  89.6 0.8 collective-permute-start.13
  90.4 0.1 copy.13.slots_ref
  90.6 4.6 %collective-permute-done.13.b_ref = f32[32,152]{1,0:T(8,128)S(1)} collective-permute-done((f32[32,152]{1,0:T(8,128)}, f32[32,152]{1,0:T(8,128)S(1)}, u32[]{:S(2)}, u32[]{:S(2)}) %collective-permute-start.13) | collective-permute-done | bytes 19488 | tf_op jit(solution)/shard_map/ppermute | solution.py:18
  95.2 0.6 copy-done.33
  95.9 1.4 add.31.coarse_ref
  97.3 0.9 copy-done.17
  98.2 0.9 copy-done.19
  99.1 0.9 copy-done.21
  100.0 0.9 copy-done.23
  100.9 0.8 copy-done.24
  101.7 64.8 %translate.1 = (f32[152,512]{1,0:T(8,128)}, f32[32,152]{1,0:T(8,128)}) custom-call(s32[160,544]{1,0:T(8,128)S(1)} %pad_add_fusion.idx_hbm, s32[512,9]{1,0:T(8,128)S(1)} %copy.13.slots_ref, f32[32,152]{1,0:T(8,128)S(1)} %copy-done.24, bf16[160,32,152]{2,1,0:T(8,128)(2,1)} %copy-done.5, bf16[160,32,152]{2,1,0:T(8,128)(2,1)} %copy-done.6, ...), custom_call_target="tpu_custom_call" | custom-call | tf_op jit(solution)/shard_map/translate/pallas_call | solution.py:236
  (63 shorter events, 0.2 us)
Async XLA Ops:
  0.6 84.0 %collective-permute-start.12 = (bf16[152,512]{1,0:T(8,128)(2,1)}, bf16[152,512]{1,0:T(8,128)(2,1)S(1)}, u32[]{:S(2)}, u32[]{:S(2)}) collective-permute-start(bf16[152,512]{1,0:T(8,128)(2,1)} %rest_5_.1), channel_id=1, source_target_pairs={{0,4},{1,5},{2,6},{3,7},{4,0},{5,1},{6,2},{7,3},{8,12},{9,13},{10,... | collective-permute-start | bytes 466952 | tf_op jit(solution)/shard_map/ppermute | solution.py:18
  2.0 82.7 %collective-permute-start.11 = (bf16[152,512]{1,0:T(8,128)(2,1)}, bf16[152,512]{1,0:T(8,128)(2,1)S(1)}, u32[]{:S(2)}, u32[]{:S(2)}) collective-permute-start(bf16[152,512]{1,0:T(8,128)(2,1)} %rest_5_.1), channel_id=1, source_target_pairs={{0,64},{8,72},{16,80},{24,88},{32,96},{40,104},{48,112},{56,120},{... | collective-permute-start | bytes 466952 | tf_op jit(solution)/shard_map/ppermute | solution.py:18
  3.4 66.8 %collective-permute-start.6 = (bf16[152,512]{1,0:T(8,128)(2,1)}, bf16[152,512]{1,0:T(8,128)(2,1)S(1)}, u32[]{:S(2)}, u32[]{:S(2)}) collective-permute-start(bf16[152,512]{1,0:T(8,128)(2,1)} %rest_5_.1), channel_id=1, source_target_pairs={{0,16},{8,24},{16,0},{24,8},{32,48},{40,56},{48,32},{56,40},{64,80... | collective-permute-start | bytes 466952 | tf_op jit(solution)/shard_map/ppermute | solution.py:18
  6.7 64.5 %collective-permute-start.5 = (bf16[152,512]{1,0:T(8,128)(2,1)}, bf16[152,512]{1,0:T(8,128)(2,1)S(1)}, u32[]{:S(2)}, u32[]{:S(2)}) collective-permute-start(bf16[152,512]{1,0:T(8,128)(2,1)} %rest_5_.1), channel_id=1, source_target_pairs={{0,32},{8,40},{16,48},{24,56},{32,0},{40,8},{48,16},{56,24},{64,96... | collective-permute-start | bytes 466952 | tf_op jit(solution)/shard_map/ppermute | solution.py:18
  16.3 7.4 %collective-permute-start = (f32[32,152]{1,0:T(8,128)}, f32[32,152]{1,0:T(8,128)S(1)}, u32[]{:S(2)}, u32[]{:S(2)}) collective-permute-start(f32[32,152]{1,0:T(8,128)} %upward.1.a_ref), channel_id=1, source_target_pairs={{0,1},{1,0},{2,3},{3,2},{4,5},{5,4},{6,7},{7,6},{8,9},{9,8},{10,11... | collective-permute-start | bytes 58376 | tf_op jit(solution)/shard_map/ppermute | solution.py:18
  16.3 4.4 %copy-start = (bf16[160,152,152]{0,2,1:T(8,128)(2,1)S(1)}, bf16[160,152,152]{0,2,1:T(8,128)(2,1)}, u32[]{:S(2)}) copy-start(bf16[160,152,152]{0,2,1:T(8,128)(2,1)} %param.8) | copy-start | bytes 22179844
  22.2 1.5 copy-start.5
  23.7 0.6 copy-start.27
  25.7 7.4 %collective-permute-start.1 = (f32[32,152]{1,0:T(8,128)}, f32[32,152]{1,0:T(8,128)S(1)}, u32[]{:S(2)}, u32[]{:S(2)}) collective-permute-start(f32[32,152]{1,0:T(8,128)} %add.24.a_ref), channel_id=1, source_target_pairs={{0,2},{1,3},{2,0},{3,1},{4,6},{5,7},{6,4},{7,5},{8,10},{9,11},{10,... | collective-permute-start | bytes 58376 | tf_op jit(solution)/shard_map/ppermute | solution.py:18
  25.7 4.4 %copy-start.1 = (bf16[160,152,152]{0,2,1:T(8,128)(2,1)S(1)}, bf16[160,152,152]{0,2,1:T(8,128)(2,1)}, u32[]{:S(2)}) copy-start(bf16[160,152,152]{0,2,1:T(8,128)(2,1)} %param.8) | copy-start | bytes 22179844
  31.6 1.5 copy-start.6
  33.1 0.6 copy-start.28
  35.1 11.0 %collective-permute-start.2 = (f32[32,152]{1,0:T(8,128)}, f32[32,152]{1,0:T(8,128)S(1)}, u32[]{:S(2)}, u32[]{:S(2)}) collective-permute-start(f32[32,152]{1,0:T(8,128)} %add.25.a_ref), channel_id=1, source_target_pairs={{0,4},{1,5},{2,6},{3,7},{4,0},{5,1},{6,2},{7,3},{8,12},{9,13},{10,... | collective-permute-start | bytes 58376 | tf_op jit(solution)/shard_map/ppermute | solution.py:18
  38.8 4.4 %copy-start.2 = (bf16[160,152,152]{0,2,1:T(8,128)(2,1)S(1)}, bf16[160,152,152]{0,2,1:T(8,128)(2,1)}, u32[]{:S(2)}) copy-start(bf16[160,152,152]{0,2,1:T(8,128)(2,1)} %param.8) | copy-start | bytes 22179844
  44.6 1.5 copy-start.7
  46.1 0.6 copy-start.29
  48.1 8.5 %collective-permute-start.3 = (f32[32,152]{1,0:T(8,128)}, f32[32,152]{1,0:T(8,128)S(1)}, u32[]{:S(2)}, u32[]{:S(2)}) collective-permute-start(f32[32,152]{1,0:T(8,128)} %add.26.a_ref), channel_id=1, source_target_pairs={{0,8},{8,0},{16,24},{24,16},{32,40},{40,32},{48,56},{56,48},{64,72... | collective-permute-start | bytes 58376 | tf_op jit(solution)/shard_map/ppermute | solution.py:18
  49.2 4.4 %copy-start.3 = (bf16[160,152,152]{0,2,1:T(8,128)(2,1)S(1)}, bf16[160,152,152]{0,2,1:T(8,128)(2,1)}, u32[]{:S(2)}) copy-start(bf16[160,152,152]{0,2,1:T(8,128)(2,1)} %param.8) | copy-start | bytes 22179844
  55.0 1.6 copy-start.8
  56.6 3.5 %copy-start.25 = (s32[160,512]{1,0:T(8,128)S(1)}, s32[160,512]{1,0:T(8,128)}, u32[]{:S(2)}) copy-start(s32[160,512]{1,0:T(8,128)} %param.9) | copy-start | bytes 983044
  56.6 3.5 %copy-start.31 = (s32[160,32]{0,1:T(8,128)S(1)}, s32[160,32]{0,1:T(8,128)}, u32[]{:S(2)}) copy-start(s32[160,32]{0,1:T(8,128)} %param.11) | copy-start | bytes 61444
  56.6 0.6 copy-start.30
  58.6 8.8 %collective-permute-start.4 = (f32[32,152]{1,0:T(8,128)}, f32[32,152]{1,0:T(8,128)S(1)}, u32[]{:S(2)}, u32[]{:S(2)}) collective-permute-start(f32[32,152]{1,0:T(8,128)} %add.27.a_ref), channel_id=1, source_target_pairs={{0,16},{8,24},{16,0},{24,8},{32,48},{40,56},{48,32},{56,40},{64,80... | collective-permute-start | bytes 58376 | tf_op jit(solution)/shard_map/ppermute | solution.py:18
  60.2 4.4 %copy-start.4 = (bf16[160,152,152]{0,2,1:T(8,128)(2,1)S(1)}, bf16[160,152,152]{0,2,1:T(8,128)(2,1)}, u32[]{:S(2)}) copy-start(bf16[160,152,152]{0,2,1:T(8,128)(2,1)} %param.8) | copy-start | bytes 22179844
  64.6 2.8 %copy-start.15 = (bf16[152,512]{1,0:T(8,128)(2,1)S(1)}, bf16[152,512]{1,0:T(8,128)(2,1)}, u32[]{:S(2)}) copy-start(bf16[152,512]{1,0:T(8,128)(2,1)} %rest_5_.1) | copy-start | bytes 466948
  66.0 1.3 copy-start.9
  67.4 23.1 %copy-start.35 = (s32[1,8,512]{2,1,0:T(8,128)S(1)}, s32[1,8,512]{2,1,0:T(8,128)}, u32[]{:S(2)}) copy-start(s32[1,8,512]{2,1,0:T(8,128)} %param.10) | copy-start | bytes 49156
  67.4 3.9 %copy-start.26 = (f32[32,152]{1,0:T(8,128)}, f32[32,152]{1,0:T(8,128)S(1)}, u32[]{:S(2)}) copy-start(f32[32,152]{1,0:T(8,128)S(1)} %collective-permute-done.4.b_ref) | copy-start | bytes 58372
  67.4 29.9 %copy-start.10 = (bf16[160,24,152]{2,1,0:T(8,128)(2,1)S(1)}, bf16[160,24,152]{2,1,0:T(8,128)(2,1)}, u32[]{:S(2)}) copy-start(bf16[160,24,152]{2,1,0:T(8,128)(2,1)} %copy-done.9) | copy-start | bytes 3502084
  67.4 6.9 %collective-permute-start.9 = (bf16[152,512]{1,0:T(8,128)(2,1)S(1)}, bf16[152,512]{1,0:T(8,128)(2,1)S(1)}, u32[]{:S(2)}, u32[]{:S(2)}) collective-permute-start(bf16[152,512]{1,0:T(8,128)(2,1)S(1)} %copy-done.15), channel_id=1, source_target_pairs={{0,128},{8,136},{16,144},{24,152},{32,160},{40,168},{48,176},{56,1... | collective-permute-start | bytes 466952 | tf_op jit(solution)/shard_map/ppermute | solution.py:18
  70.2 1.0 copy-start.11
  70.2 5.6 %collective-permute-start.8 = (bf16[152,512]{1,0:T(8,128)(2,1)S(1)}, bf16[152,512]{1,0:T(8,128)(2,1)S(1)}, u32[]{:S(2)}, u32[]{:S(2)}) collective-permute-start(bf16[152,512]{1,0:T(8,128)(2,1)S(1)} %copy-done.15), channel_id=1, source_target_pairs={{0,8},{8,0},{16,24},{24,16},{32,40},{40,32},{48,56},{56,48},{64,72... | collective-permute-start | bytes 466952 | tf_op jit(solution)/shard_map/ppermute | solution.py:18
  71.2 0.7 copy-start.13
  73.3 24.0 %copy-start.12 = (bf16[152,512]{1,0:T(8,128)(2,1)S(1)}, bf16[152,512]{1,0:T(8,128)(2,1)}, u32[]{:S(2)}) copy-start(bf16[152,512]{1,0:T(8,128)(2,1)} %copy-done.11) | copy-start | bytes 466948
  73.3 24.0 %copy-start.14 = (bf16[152,512]{1,0:T(8,128)(2,1)S(1)}, bf16[152,512]{1,0:T(8,128)(2,1)}, u32[]{:S(2)}) copy-start(bf16[152,512]{1,0:T(8,128)(2,1)} %copy-done.13) | copy-start | bytes 466948
  73.3 8.2 %collective-permute-start.7 = (f32[32,152]{1,0:T(8,128)}, f32[32,152]{1,0:T(8,128)S(1)}, u32[]{:S(2)}, u32[]{:S(2)}) collective-permute-start(f32[32,152]{1,0:T(8,128)} %add.28.a_ref), channel_id=1, source_target_pairs={{0,32},{8,40},{16,48},{24,56},{32,0},{40,8},{48,16},{56,24},{64,96... | collective-permute-start | bytes 58376 | tf_op jit(solution)/shard_map/ppermute | solution.py:18
  74.3 7.2 %copy-start.20 = (bf16[152,512]{1,0:T(8,128)(2,1)}, bf16[152,512]{1,0:T(8,128)(2,1)S(1)}, u32[]{:S(2)}) copy-start(bf16[152,512]{1,0:T(8,128)(2,1)S(1)} %collective-permute-done.9.rest_1_.rest_13_) | copy-start | bytes 466948
  74.3 16.3 %collective-permute-start.14 = (bf16[152,512]{1,0:T(8,128)(2,1)S(1)}, bf16[152,512]{1,0:T(8,128)(2,1)}, u32[]{:S(2)}, u32[]{:S(2)}) collective-permute-start(bf16[152,512]{1,0:T(8,128)(2,1)S(1)} %copy-done.15), channel_id=1, source_target_pairs={{0,2},{1,3},{2,0},{3,1},{4,6},{5,7},{6,4},{7,5},{8,10},{9,11},{10,... | collective-permute-start | bytes 466952 | tf_op jit(solution)/shard_map/ppermute | solution.py:18
  75.8 5.7 %copy-start.22 = (bf16[152,512]{1,0:T(8,128)(2,1)}, bf16[152,512]{1,0:T(8,128)(2,1)S(1)}, u32[]{:S(2)}) copy-start(bf16[152,512]{1,0:T(8,128)(2,1)S(1)} %collective-permute-done.8.rest_0_.rest_9_) | copy-start | bytes 466948
  75.8 14.8 %collective-permute-start.15 = (bf16[152,512]{1,0:T(8,128)(2,1)S(1)}, bf16[152,512]{1,0:T(8,128)(2,1)}, u32[]{:S(2)}, u32[]{:S(2)}) collective-permute-start(bf16[152,512]{1,0:T(8,128)(2,1)S(1)} %copy-done.15), channel_id=1, source_target_pairs={{0,1},{1,0},{2,3},{3,2},{4,5},{5,4},{6,7},{7,6},{8,9},{9,8},{10,11... | collective-permute-start | bytes 466952 | tf_op jit(solution)/shard_map/ppermute | solution.py:18
  81.5 0.6 copy-start.32
  83.5 4.1 %collective-permute-start.10 = (f32[32,152]{1,0:T(8,128)}, f32[32,152]{1,0:T(8,128)S(1)}, u32[]{:S(2)}, u32[]{:S(2)}) collective-permute-start(f32[32,152]{1,0:T(8,128)} %add.29.a_ref), channel_id=1, source_target_pairs={{0,64},{8,72},{16,80},{24,88},{32,96},{40,104},{48,112},{56,120},{... | collective-permute-start | bytes 58376 | tf_op jit(solution)/shard_map/ppermute | solution.py:18
  84.6 3.0 %copy-start.16 = (bf16[152,512]{1,0:T(8,128)(2,1)}, bf16[152,512]{1,0:T(8,128)(2,1)S(1)}, u32[]{:S(2)}) copy-start(bf16[152,512]{1,0:T(8,128)(2,1)S(1)} %collective-permute-done.12.rest_1_.rest_8_) | copy-start | bytes 466948
  84.6 3.0 %copy-start.18 = (bf16[152,512]{1,0:T(8,128)(2,1)}, bf16[152,512]{1,0:T(8,128)(2,1)S(1)}, u32[]{:S(2)}) copy-start(bf16[152,512]{1,0:T(8,128)(2,1)S(1)} %collective-permute-done.11.rest_0_.rest_12_) | copy-start | bytes 466948
  87.6 0.6 copy-start.34
  89.6 5.6 %collective-permute-start.13 = (f32[32,152]{1,0:T(8,128)}, f32[32,152]{1,0:T(8,128)S(1)}, u32[]{:S(2)}, u32[]{:S(2)}) collective-permute-start(f32[32,152]{1,0:T(8,128)} %add.30.a_ref), channel_id=1, source_target_pairs={{0,128},{8,136},{16,144},{24,152},{32,160},{40,168},{48,176},{56,1... | collective-permute-start | bytes 58376 | tf_op jit(solution)/shard_map/ppermute | solution.py:18
  95.2 0.6 copy-start.33
  97.3 0.9 copy-start.17
  98.2 0.9 copy-start.19
  99.1 0.9 copy-start.21
  100.0 0.9 copy-start.23
  100.9 0.8 copy-start.24

commit v4 on v3

--- a/solution.py
+++ b/solution.py
@@ -60,6 +60,7 @@
     )(place, fine_mult, up_operators)
 
 
+SETTLED = 4
 STRIP = 16
 PIECE = 32
 GROUP = 2
@@ -96,28 +97,12 @@
         out_specs=pl.BlockSpec((offsets, STRIP, surface), lambda step: (0, step, 0)),
         out_shape=jax.ShapeDtypeStruct((offsets, count, surface), jnp.bfloat16),
         scratch_shapes=[pltpu.VMEM((offsets * (STRIP + 1), LANES), jnp.float32) for _ in range(2)],
-        compiler_params=pltpu.CompilerParams(vmem_limit_bytes=16 << 20),
+        compiler_params=pltpu.CompilerParams(vmem_limit_bytes=60 << 20),
         cost_estimate=pl.CostEstimate(
             flops=2 * offsets * offsets * count * surface, bytes_accessed=6 * offsets * count * surface, transcendentals=0
         ),
         name="relayout",
     )(far_turned)
-
-
-def add_kernel(a_ref, b_ref, *rest):
-    rest[-1][...] = a_ref[...] + b_ref[...]
-
-
-def add_after(a, b, others):
-    vmem = pl.BlockSpec(memory_space=pltpu.VMEM)
-    return pl.pallas_call(
-        add_kernel,
-        in_specs=[vmem, vmem] + [pl.BlockSpec(memory_space=pl.ANY) for _ in others],
-        out_specs=vmem,
-        out_shape=jax.ShapeDtypeStruct(a.shape, a.dtype),
-        cost_estimate=pl.CostEstimate(flops=a.size, bytes_accessed=12 * a.size, transcendentals=0),
-        name="add",
-    )(a, b, *others)
 
 
 def translate_kernel(sections, pieces, idx_hbm, slots_ref, coarse_ref, *rest):
@@ -256,7 +241,7 @@
         ]
         + [pltpu.SMEM((GROUP, targets), jnp.int32) for _ in range(PHASES)]
         + [pltpu.SemaphoreType.DMA((PHASES, GROUP))],
-        compiler_params=pltpu.CompilerParams(vmem_limit_bytes=48 << 20),
+        compiler_params=pltpu.CompilerParams(vmem_limit_bytes=51 << 20),
         name="translate",
     )(idx, slots, coarse, *far_pieces, *blocks)
 
@@ -269,17 +254,19 @@
     bits = [("hy", bit) for bit in range(bits_y)] + [("hx", bit) for bit in range(bits_x)]
     order = bits[bits_y : bits_y + 3][::-1] + bits[bits_y + 3 :][::-1] + bits[:bits_y][::-1]
     ghosts = {bit: from_partner(fine_mult, *bit) for bit in order}
-    blocks = [fine_mult] + [ghosts[bit] for bit in bits]
-    sections = len(blocks)
+    sections = len(bits) + 1
     place = jnp.stack([lax.axis_index("hx"), lax.axis_index("hy")]).astype(jnp.int32)
     coarse = upward(place, coarse_boxes, fine_mult, up_operators)
     far_turned = jnp.transpose(far_operators, (1, 2, 0))
     pieces = [relayout(far_turned, piece) for piece in range(-(-surface // PIECE))]
-    due = [[piece] for piece in pieces] + [[] for _ in range(len(bits) - len(pieces))]
-    for number, bit in enumerate(order):
-        due[min(4 + number // 2, len(bits) - 1)].append(ghosts[bit])
-    for bit, others in zip(bits, due):
-        coarse = add_after(coarse, from_partner(coarse, *bit), others)
+    for number, bit in enumerate(bits):
+        coarse = coarse + from_partner(coarse, *bit)
+        if number < len(pieces):
+            coarse, pieces[number] = lax.optimization_barrier((coarse, pieces[number]))
+        if SETTLED <= number < len(bits) - 1:
+            for other in order[2 * (number - SETTLED) : 2 * (number - SETTLED) + 2]:
+                coarse, ghosts[other] = lax.optimization_barrier((coarse, ghosts[other]))
+    blocks = [fine_mult] + [ghosts[bit] for bit in bits]
     first_coarse = sections * boxes
     zero_row = first_coarse + coarse_boxes
     idx = jnp.concatenate(

time: 168 us -> 129 us (0.77)
  the two profiles are of different devices: /device:TPU:24 before, /device:TPU:1 now
where the time goes in v4:
time: 129 us
  Pallas kernels  86.7 us (67%)
  starting transfers between devices  26.9 us (21%)
  waiting for transfers between devices  13.3 us (10%)
    pallas_call x1, Pallas kernels, translate(): pl.pallas_call(functools.partial(translate_kernel, sections, len(far_piec...  64.7 us
    ppermute x16, starting transfers between devices, from_partner(): return lax.ppermute(value, axis, pairs)  26.9 us
    pallas_call x5, Pallas kernels, relayout(): pl.pallas_call(relayout_kernel, grid=(-(-count // STRIP),), in_specs=[pl....  18.4 us
    ppermute x16, waiting for transfers between devices, from_partner(): return lax.ppermute(value, axis, pairs)  13.3 us
    pallas_call x1, Pallas kernels, upward(): pl.pallas_call(upward_kernel, in_specs=[pl.BlockSpec(memory_space=pltpu.S...  3.58 us
  transfers between devices with their start and end apart: 16, of which 3 were waited for; matrix products, arithmetic and copies ran while one was open for 1% of the time, Pallas kernels for 17%

profile of v4, /device:TPU:1, one launch (start us, length us, event | category | flops | bytes accessed | tf_op | source)
XLA Modules:
  0.0 128.8 jit_solution(16638850011988340124)
XLA Ops:
  0.6 3.8 %collective-permute-start.12 = (bf16[152,512]{1,0:T(8,128)(2,1)}, bf16[152,512]{1,0:T(8,128)(2,1)S(1)}, u32[]{:S(2)}, u32[]{:S(2)}) collective-permute-start(bf16[152,512]{1,0:T(8,128)(2,1)} %rest_5_.1), channel_id=1, source_target_pairs={{0,4},{1,5},{2,6},{3,7},{4,0},{5,1},{6,2},{7,3},{8,12},{9,13},{10,... | collective-permute-start | bytes 466952 | tf_op jit(solution)/shard_map/ppermute | solution.py:18
  4.5 1.2 collective-permute-start.11
  5.7 3.0 %collective-permute-start.6 = (bf16[152,512]{1,0:T(8,128)(2,1)}, bf16[152,512]{1,0:T(8,128)(2,1)S(1)}, u32[]{:S(2)}, u32[]{:S(2)}) collective-permute-start(bf16[152,512]{1,0:T(8,128)(2,1)} %rest_5_.1), channel_id=1, source_target_pairs={{0,16},{8,24},{16,0},{24,8},{32,48},{40,56},{48,32},{56,40},{64,80... | collective-permute-start | bytes 466952 | tf_op jit(solution)/shard_map/ppermute | solution.py:18
  8.7 5.1 %collective-permute-start.5 = (bf16[152,512]{1,0:T(8,128)(2,1)}, bf16[152,512]{1,0:T(8,128)(2,1)S(1)}, u32[]{:S(2)}, u32[]{:S(2)}) collective-permute-start(bf16[152,512]{1,0:T(8,128)(2,1)} %rest_5_.1), channel_id=1, source_target_pairs={{0,32},{8,40},{16,48},{24,56},{32,0},{40,8},{48,16},{56,24},{64,96... | collective-permute-start | bytes 466952 | tf_op jit(solution)/shard_map/ppermute | solution.py:18
  13.8 0.6 pad_add_fusion.2.place_ref
  14.4 3.6 %upward.1 = f32[32,152]{1,0:T(8,128)} custom-call(s32[2]{0:T(128)} %pad_add_fusion.2.place_ref, bf16[152,512]{1,0:T(8,128)(2,1)} %rest_5_.1, bf16[8,152,152]{2,1,0:T(8,128)(2,1)} %up_ref.1), custom_call_target="tpu_custom_call" | custom-call | tf_op jit(solution)/shard_map/upward/pallas_call | solution.py:53
  18.0 1.8 %collective-permute-start = (f32[32,152]{1,0:T(8,128)}, f32[32,152]{1,0:T(8,128)S(1)}, u32[]{:S(2)}, u32[]{:S(2)}) collective-permute-start(f32[32,152]{1,0:T(8,128)} %upward.1), channel_id=1, source_target_pairs={{0,1},{1,0},{2,3},{3,2},{4,5},{5,4},{6,7},{7,6},{8,9},{9,8},{10,11... | collective-permute-start | bytes 58376 | tf_op jit(solution)/shard_map/ppermute | solution.py:18
  19.8 0.0 copy-start.2
  19.8 3.8 %relayout.5.rest_0_ = bf16[160,32,152]{2,1,0:T(8,128)(2,1)} custom-call(bf16[152,152,160]{2,1,0:T(8,128)(2,1)} %bitcast.7), custom_call_target="tpu_custom_call" | custom-call | flops 249036800 | bytes 4669440 | tf_op jit(solution)/shard_map/relayout/pallas_call | solution.py:93
  23.5 0.0 collective-permute-done
  23.5 0.0 copy-done.2
  23.5 0.5 collective-permute-start.1
  24.0 3.7 %relayout.6.rest_1_ = bf16[160,32,152]{2,1,0:T(8,128)(2,1)} custom-call(bf16[152,152,160]{2,1,0:T(8,128)(2,1)} %bitcast.8), custom_call_target="tpu_custom_call" | custom-call | flops 249036800 | bytes 4669440 | tf_op jit(solution)/shard_map/relayout/pallas_call | solution.py:93
  27.7 0.0 collective-permute-done.1
  27.7 1.6 %collective-permute-start.2 = (f32[32,152]{1,0:T(8,128)S(1)}, f32[32,152]{1,0:T(8,128)S(1)}, u32[]{:S(2)}, u32[]{:S(2)}) collective-permute-start(f32[32,152]{1,0:T(8,128)S(1)} %add.33), channel_id=1, source_target_pairs={{0,4},{1,5},{2,6},{3,7},{4,0},{5,1},{6,2},{7,3},{8,12},{9,13},{10,... | collective-permute-start | bytes 58376 | tf_op jit(solution)/shard_map/ppermute | solution.py:18
  29.4 3.7 %relayout.7.rest_2_ = bf16[160,32,152]{2,1,0:T(8,128)(2,1)} custom-call(bf16[152,152,160]{2,1,0:T(8,128)(2,1)} %bitcast.9), custom_call_target="tpu_custom_call" | custom-call | flops 249036800 | bytes 4669440 | tf_op jit(solution)/shard_map/relayout/pallas_call | solution.py:93
  33.1 0.0 collective-permute-done.2
  33.1 0.0 copy-start.1
  33.1 0.0 copy-start.3
  33.1 0.8 collective-permute-start.3
  33.9 3.7 %relayout.8.rest_3_ = bf16[160,32,152]{2,1,0:T(8,128)(2,1)} custom-call(bf16[152,152,160]{2,1,0:T(8,128)(2,1)} %bitcast.10), custom_call_target="tpu_custom_call" | custom-call | flops 249036800 | bytes 4669440 | tf_op jit(solution)/shard_map/relayout/pallas_call | solution.py:93
  37.6 0.0 collective-permute-done.3
  37.6 1.3 collective-permute-start.4
  38.9 0.0 copy-done.1
  38.9 0.0 copy-done.3
  39.0 0.1 copy.11
  39.1 0.0 copy-start
  39.1 0.0 copy-start.4
  39.1 3.6 %relayout.9.rest_4_ = bf16[160,24,152]{2,1,0:T(8,128)(2,1)} custom-call(bf16[152,152,160]{2,1,0:T(8,128)(2,1)} %bitcast.11), custom_call_target="tpu_custom_call" | custom-call | flops 186777600 | bytes 3502080 | tf_op jit(solution)/shard_map/relayout/pallas_call | solution.py:93
  42.6 0.0 collective-permute-done.4
  42.6 0.0 copy-done
  42.6 2.4 %collective-permute-start.9 = (bf16[152,512]{1,0:T(8,128)(2,1)S(1)}, bf16[152,512]{1,0:T(8,128)(2,1)S(1)}, u32[]{:S(2)}, u32[]{:S(2)}) collective-permute-start(bf16[152,512]{1,0:T(8,128)(2,1)S(1)} %copy-done), channel_id=1, source_target_pairs={{0,128},{8,136},{16,144},{24,152},{32,160},{40,168},{48,176},{56,1... | collective-permute-start | bytes 466952 | tf_op jit(solution)/shard_map/ppermute | solution.py:18
  45.1 0.0 collective-permute-done.5.rest_11_
  45.1 0.8 collective-permute-start.8
  45.9 0.0 collective-permute-done.6.rest_10_
  45.9 0.0 collective-permute-start.7
  45.9 6.7 %collective-permute-done.7 = f32[32,152]{1,0:T(8,128)S(1)} collective-permute-done((f32[32,152]{1,0:T(8,128)S(1)}, f32[32,152]{1,0:T(8,128)S(1)}, u32[]{:S(2)}, u32[]{:S(2)}) %collective-permute-start.7) | collective-permute-done | bytes 19488 | tf_op jit(solution)/shard_map/ppermute | solution.py:18
  52.6 2.8 %collective-permute-start.14 = (bf16[152,512]{1,0:T(8,128)(2,1)S(1)}, bf16[152,512]{1,0:T(8,128)(2,1)S(1)}, u32[]{:S(2)}, u32[]{:S(2)}) collective-permute-start(bf16[152,512]{1,0:T(8,128)(2,1)S(1)} %copy-done), channel_id=1, source_target_pairs={{0,1},{1,0},{2,3},{3,2},{4,5},{5,4},{6,7},{7,6},{8,9},{9,8},{10,11... | collective-permute-start | bytes 466952 | tf_op jit(solution)/shard_map/ppermute | solution.py:18
  55.4 0.0 collective-permute-done.8.rest_9_
  55.4 1.0 collective-permute-start.15
  56.5 0.0 collective-permute-done.9.rest_13_
  56.5 0.0 collective-permute-start.10
  56.5 3.0 %collective-permute-done.10 = f32[32,152]{1,0:T(8,128)S(1)} collective-permute-done((f32[32,152]{1,0:T(8,128)S(1)}, f32[32,152]{1,0:T(8,128)S(1)}, u32[]{:S(2)}, u32[]{:S(2)}) %collective-permute-start.10) | collective-permute-done | bytes 19488 | tf_op jit(solution)/shard_map/ppermute | solution.py:18
  59.6 0.0 collective-permute-done.11.rest_12_
  59.6 0.0 collective-permute-done.12.rest_8_
  59.6 0.6 collective-permute-start.13
  60.2 0.0 copy-done.4
  60.2 0.1 copy.13.slots_ref
  60.3 3.6 %collective-permute-done.13 = f32[32,152]{1,0:T(8,128)S(1)} collective-permute-done((f32[32,152]{1,0:T(8,128)S(1)}, f32[32,152]{1,0:T(8,128)S(1)}, u32[]{:S(2)}, u32[]{:S(2)}) %collective-permute-start.13) | collective-permute-done | bytes 19488 | tf_op jit(solution)/shard_map/ppermute | solution.py:18
  63.9 0.0 collective-permute-done.14.rest_6_
  63.9 0.0 collective-permute-done.15.rest_7_
  64.0 64.7 %translate.1 = (f32[152,512]{1,0:T(8,128)}, f32[32,152]{1,0:T(8,128)}) custom-call(s32[160,544]{1,0:T(8,128)S(1)} %pad_add_fusion.idx_hbm, s32[512,9]{1,0:T(8,128)S(1)} %copy.13.slots_ref, f32[32,152]{1,0:T(8,128)S(1)} %add.39.coarse_ref, bf16[160,32,152]{2,1,0:T(8,128)(2,1)} %relayout.5.rest_0_, bf16[160,32,152]{2,1,0:T(8,128)(2,1)} %relayout.6.rest_1_, ...), custom_call_target="tpu_custom_call" | custom-call | tf_op jit(solution)/shard_map/translate/pallas_call | solution.py:221
  (13 shorter events, 0.1 us)
Async XLA Ops:
  0.6 58.9 %collective-permute-start.12 = (bf16[152,512]{1,0:T(8,128)(2,1)}, bf16[152,512]{1,0:T(8,128)(2,1)S(1)}, u32[]{:S(2)}, u32[]{:S(2)}) collective-permute-start(bf16[152,512]{1,0:T(8,128)(2,1)} %rest_5_.1), channel_id=1, source_target_pairs={{0,4},{1,5},{2,6},{3,7},{4,0},{5,1},{6,2},{7,3},{8,12},{9,13},{10,... | collective-permute-start | bytes 466952 | tf_op jit(solution)/shard_map/ppermute | solution.py:18
  4.5 55.1 %collective-permute-start.11 = (bf16[152,512]{1,0:T(8,128)(2,1)}, bf16[152,512]{1,0:T(8,128)(2,1)S(1)}, u32[]{:S(2)}, u32[]{:S(2)}) collective-permute-start(bf16[152,512]{1,0:T(8,128)(2,1)} %rest_5_.1), channel_id=1, source_target_pairs={{0,64},{8,72},{16,80},{24,88},{32,96},{40,104},{48,112},{56,120},{... | collective-permute-start | bytes 466952 | tf_op jit(solution)/shard_map/ppermute | solution.py:18
  5.7 40.3 %collective-permute-start.6 = (bf16[152,512]{1,0:T(8,128)(2,1)}, bf16[152,512]{1,0:T(8,128)(2,1)S(1)}, u32[]{:S(2)}, u32[]{:S(2)}) collective-permute-start(bf16[152,512]{1,0:T(8,128)(2,1)} %rest_5_.1), channel_id=1, source_target_pairs={{0,16},{8,24},{16,0},{24,8},{32,48},{40,56},{48,32},{56,40},{64,80... | collective-permute-start | bytes 466952 | tf_op jit(solution)/shard_map/ppermute | solution.py:18
  8.7 36.4 %collective-permute-start.5 = (bf16[152,512]{1,0:T(8,128)(2,1)}, bf16[152,512]{1,0:T(8,128)(2,1)S(1)}, u32[]{:S(2)}, u32[]{:S(2)}) collective-permute-start(bf16[152,512]{1,0:T(8,128)(2,1)} %rest_5_.1), channel_id=1, source_target_pairs={{0,32},{8,40},{16,48},{24,56},{32,0},{40,8},{48,16},{56,24},{64,96... | collective-permute-start | bytes 466952 | tf_op jit(solution)/shard_map/ppermute | solution.py:18
  18.0 5.6 %collective-permute-start = (f32[32,152]{1,0:T(8,128)}, f32[32,152]{1,0:T(8,128)S(1)}, u32[]{:S(2)}, u32[]{:S(2)}) collective-permute-start(f32[32,152]{1,0:T(8,128)} %upward.1), channel_id=1, source_target_pairs={{0,1},{1,0},{2,3},{3,2},{4,5},{5,4},{6,7},{7,6},{8,9},{9,8},{10,11... | collective-permute-start | bytes 58376 | tf_op jit(solution)/shard_map/ppermute | solution.py:18
  19.8 3.8 %copy-start.2 = (f32[32,152]{1,0:T(8,128)S(1)}, f32[32,152]{1,0:T(8,128)}, u32[]{:S(2)}) copy-start(f32[32,152]{1,0:T(8,128)} %upward.1) | copy-start | bytes 58372
  23.5 4.2 %collective-permute-start.1 = (f32[32,152]{1,0:T(8,128)S(1)}, f32[32,152]{1,0:T(8,128)S(1)}, u32[]{:S(2)}, u32[]{:S(2)}) collective-permute-start(f32[32,152]{1,0:T(8,128)S(1)} %add.32), channel_id=1, source_target_pairs={{0,2},{1,3},{2,0},{3,1},{4,6},{5,7},{6,4},{7,5},{8,10},{9,11},{10,... | collective-permute-start | bytes 58376 | tf_op jit(solution)/shard_map/ppermute | solution.py:18
  27.7 5.3 %collective-permute-start.2 = (f32[32,152]{1,0:T(8,128)S(1)}, f32[32,152]{1,0:T(8,128)S(1)}, u32[]{:S(2)}, u32[]{:S(2)}) collective-permute-start(f32[32,152]{1,0:T(8,128)S(1)} %add.33), channel_id=1, source_target_pairs={{0,4},{1,5},{2,6},{3,7},{4,0},{5,1},{6,2},{7,3},{8,12},{9,13},{10,... | collective-permute-start | bytes 58376 | tf_op jit(solution)/shard_map/ppermute | solution.py:18
  33.1 5.8 %copy-start.1 = (s32[160,512]{1,0:T(8,128)S(1)}, s32[160,512]{1,0:T(8,128)}, u32[]{:S(2)}) copy-start(s32[160,512]{1,0:T(8,128)} %param.9) | copy-start | bytes 983044
  33.1 5.9 %copy-start.3 = (s32[160,32]{0,1:T(8,128)S(1)}, s32[160,32]{0,1:T(8,128)}, u32[]{:S(2)}) copy-start(s32[160,32]{0,1:T(8,128)} %param.11) | copy-start | bytes 61444
  33.1 4.5 %collective-permute-start.3 = (f32[32,152]{1,0:T(8,128)S(1)}, f32[32,152]{1,0:T(8,128)S(1)}, u32[]{:S(2)}, u32[]{:S(2)}) collective-permute-start(f32[32,152]{1,0:T(8,128)S(1)} %add.34), channel_id=1, source_target_pairs={{0,8},{8,0},{16,24},{24,16},{32,40},{40,32},{48,56},{56,48},{64,72... | collective-permute-start | bytes 58376 | tf_op jit(solution)/shard_map/ppermute | solution.py:18
  37.6 5.0 %collective-permute-start.4 = (f32[32,152]{1,0:T(8,128)S(1)}, f32[32,152]{1,0:T(8,128)S(1)}, u32[]{:S(2)}, u32[]{:S(2)}) collective-permute-start(f32[32,152]{1,0:T(8,128)S(1)} %add.35), channel_id=1, source_target_pairs={{0,16},{8,24},{16,0},{24,8},{32,48},{40,56},{48,32},{56,40},{64,80... | collective-permute-start | bytes 58376 | tf_op jit(solution)/shard_map/ppermute | solution.py:18
  39.1 3.6 %copy-start = (bf16[152,512]{1,0:T(8,128)(2,1)S(1)}, bf16[152,512]{1,0:T(8,128)(2,1)}, u32[]{:S(2)}) copy-start(bf16[152,512]{1,0:T(8,128)(2,1)} %rest_5_.1) | copy-start | bytes 466948
  39.1 21.1 %copy-start.4 = (s32[1,8,512]{2,1,0:T(8,128)S(1)}, s32[1,8,512]{2,1,0:T(8,128)}, u32[]{:S(2)}) copy-start(s32[1,8,512]{2,1,0:T(8,128)} %param.10) | copy-start | bytes 49156
  42.6 13.9 %collective-permute-start.9 = (bf16[152,512]{1,0:T(8,128)(2,1)S(1)}, bf16[152,512]{1,0:T(8,128)(2,1)S(1)}, u32[]{:S(2)}, u32[]{:S(2)}) collective-permute-start(bf16[152,512]{1,0:T(8,128)(2,1)S(1)} %copy-done), channel_id=1, source_target_pairs={{0,128},{8,136},{16,144},{24,152},{32,160},{40,168},{48,176},{56,1... | collective-permute-start | bytes 466952 | tf_op jit(solution)/shard_map/ppermute | solution.py:18
  45.1 10.3 %collective-permute-start.8 = (bf16[152,512]{1,0:T(8,128)(2,1)S(1)}, bf16[152,512]{1,0:T(8,128)(2,1)S(1)}, u32[]{:S(2)}, u32[]{:S(2)}) collective-permute-start(bf16[152,512]{1,0:T(8,128)(2,1)S(1)} %copy-done), channel_id=1, source_target_pairs={{0,8},{8,0},{16,24},{24,16},{32,40},{40,32},{48,56},{56,48},{64,72... | collective-permute-start | bytes 466952 | tf_op jit(solution)/shard_map/ppermute | solution.py:18
  45.9 6.7 %collective-permute-start.7 = (f32[32,152]{1,0:T(8,128)S(1)}, f32[32,152]{1,0:T(8,128)S(1)}, u32[]{:S(2)}, u32[]{:S(2)}) collective-permute-start(f32[32,152]{1,0:T(8,128)S(1)} %add.36), channel_id=1, source_target_pairs={{0,32},{8,40},{16,48},{24,56},{32,0},{40,8},{48,16},{56,24},{64,96... | collective-permute-start | bytes 58376 | tf_op jit(solution)/shard_map/ppermute | solution.py:18
  52.6 11.3 %collective-permute-start.14 = (bf16[152,512]{1,0:T(8,128)(2,1)S(1)}, bf16[152,512]{1,0:T(8,128)(2,1)S(1)}, u32[]{:S(2)}, u32[]{:S(2)}) collective-permute-start(bf16[152,512]{1,0:T(8,128)(2,1)S(1)} %copy-done), channel_id=1, source_target_pairs={{0,1},{1,0},{2,3},{3,2},{4,5},{5,4},{6,7},{7,6},{8,9},{9,8},{10,11... | collective-permute-start | bytes 466952 | tf_op jit(solution)/shard_map/ppermute | solution.py:18
  55.4 8.5 %collective-permute-start.15 = (bf16[152,512]{1,0:T(8,128)(2,1)S(1)}, bf16[152,512]{1,0:T(8,128)(2,1)S(1)}, u32[]{:S(2)}, u32[]{:S(2)}) collective-permute-start(bf16[152,512]{1,0:T(8,128)(2,1)S(1)} %copy-done), channel_id=1, source_target_pairs={{0,2},{1,3},{2,0},{3,1},{4,6},{5,7},{6,4},{7,5},{8,10},{9,11},{10,... | collective-permute-start | bytes 466952 | tf_op jit(solution)/shard_map/ppermute | solution.py:18
  56.5 3.1 %collective-permute-start.10 = (f32[32,152]{1,0:T(8,128)S(1)}, f32[32,152]{1,0:T(8,128)S(1)}, u32[]{:S(2)}, u32[]{:S(2)}) collective-permute-start(f32[32,152]{1,0:T(8,128)S(1)} %add.37), channel_id=1, source_target_pairs={{0,64},{8,72},{16,80},{24,88},{32,96},{40,104},{48,112},{56,120},{... | collective-permute-start | bytes 58376 | tf_op jit(solution)/shard_map/ppermute | solution.py:18
  59.6 4.4 %collective-permute-start.13 = (f32[32,152]{1,0:T(8,128)S(1)}, f32[32,152]{1,0:T(8,128)S(1)}, u32[]{:S(2)}, u32[]{:S(2)}) collective-permute-start(f32[32,152]{1,0:T(8,128)S(1)} %add.38), channel_id=1, source_target_pairs={{0,128},{8,136},{16,144},{24,152},{32,160},{40,168},{48,176},{56,1... | collective-permute-start | bytes 58376 | tf_op jit(solution)/shard_map/ppermute | solution.py:18

commit v5 on v4

--- a/solution.py
+++ b/solution.py
@@ -60,9 +60,8 @@
     )(place, fine_mult, up_operators)
 
 
-SETTLED = 4
+SETTLED = 3
 STRIP = 16
-PIECE = 32
 GROUP = 2
 PHASES = 8
 CHUNKS = 2
@@ -86,13 +85,12 @@
         out_ref[offset, :, LANES:] = high[span, :][:, : surface - LANES].astype(jnp.bfloat16)
 
 
-def relayout(far_turned, piece):
+def relayout(far_turned, first, strips):
     surface, _, offsets = far_turned.shape
-    count = min(PIECE, surface - piece * PIECE)
-    first = piece * PIECE // STRIP
+    count = min(strips * STRIP, surface - first * STRIP)
     return pl.pallas_call(
         relayout_kernel,
-        grid=(-(-count // STRIP),),
+        grid=(strips,),
         in_specs=[pl.BlockSpec((STRIP, surface, offsets), lambda step: (first + step, 0, 0))],
         out_specs=pl.BlockSpec((offsets, STRIP, surface), lambda step: (0, step, 0)),
         out_shape=jax.ShapeDtypeStruct((offsets, count, surface), jnp.bfloat16),
@@ -258,12 +256,14 @@
     place = jnp.stack([lax.axis_index("hx"), lax.axis_index("hy")]).astype(jnp.int32)
     coarse = upward(place, coarse_boxes, fine_mult, up_operators)
     far_turned = jnp.transpose(far_operators, (1, 2, 0))
-    pieces = [relayout(far_turned, piece) for piece in range(-(-surface // PIECE))]
-    for number, bit in enumerate(bits):
+    strips = -(-surface // STRIP)
+    cuts = [stage * strips // len(bits) for stage in range(len(bits) + 1)]
+    pieces = [relayout(far_turned, low, high - low) for low, high in zip(cuts, cuts[1:])]
+    stages = [bit for bit in bits if bit != order[0]] + [order[0]]
+    for number, bit in enumerate(stages):
         coarse = coarse + from_partner(coarse, *bit)
-        if number < len(pieces):
-            coarse, pieces[number] = lax.optimization_barrier((coarse, pieces[number]))
-        if SETTLED <= number < len(bits) - 1:
+        coarse, pieces[number] = lax.optimization_barrier((coarse, pieces[number]))
+        if SETTLED <= number < len(stages) - 1:
             for other in order[2 * (number - SETTLED) : 2 * (number - SETTLED) + 2]:
                 coarse, ghosts[other] = lax.optimization_barrier((coarse, ghosts[other]))
     blocks = [fine_mult] + [ghosts[bit] for bit in bits]

time: 129 us -> 128 us (level); the launches traced: 129 us -> 126 us
  waiting for transfers between devices: 13.3 us -> 3.24 us
  Pallas kernels: 86.7 us -> 94.2 us
    ppermute x16, waiting for transfers between devices: 13.3 us -> 3.24 us  [from_partner(): return lax.ppermute(value, axis, pairs)]
    pallas_call x5 -> x8, Pallas kernels: 18.4 us -> 25.4 us  [relayout(): pl.pallas_call(relayout_kernel, grid=(strips,), in_specs=[pl.BlockSpec((S...]
  transfers between devices with their start and end apart: 16 -> 16, of which waited for: 3 -> 2; matrix products, arithmetic and copies ran while one was open for 1% -> 1% of each run, Pallas kernels for 17% -> 23%
where the time goes in v5:
time: 128 us; the launch traced here: 126 us
  Pallas kernels  94.2 us (74%)
  starting transfers between devices  27 us (21%)
  waiting for transfers between devices  3.24 us (3%)
    pallas_call x1, Pallas kernels, translate(): pl.pallas_call(functools.partial(translate_kernel, sections, len(far_piec...  65.2 us
    ppermute x16, starting transfers between devices, from_partner(): return lax.ppermute(value, axis, pairs)  27 us
    pallas_call x8, Pallas kernels, relayout(): pl.pallas_call(relayout_kernel, grid=(strips,), in_specs=[pl.BlockSpec((S...  25.4 us
    pallas_call x1, Pallas kernels, upward(): pl.pallas_call(upward_kernel, in_specs=[pl.BlockSpec(memory_space=pltpu.S...  3.58 us
    ppermute x16, waiting for transfers between devices, from_partner(): return lax.ppermute(value, axis, pairs)  3.24 us
  transfers between devices with their start and end apart: 16, of which 2 were waited for; matrix products, arithmetic and copies ran while one was open for 1% of the time, Pallas kernels for 23%

profile of v5, /device:TPU:1, one launch (start us, length us, event | category | flops | bytes accessed | tf_op | source)
XLA Modules:
  0.0 126.4 jit_solution(16903025927093321990)
XLA Ops:
  0.6 3.9 %collective-permute-start.5 = (bf16[152,512]{1,0:T(8,128)(2,1)}, bf16[152,512]{1,0:T(8,128)(2,1)S(1)}, u32[]{:S(2)}, u32[]{:S(2)}) collective-permute-start(bf16[152,512]{1,0:T(8,128)(2,1)} %rest_8_.1), channel_id=1, source_target_pairs={{0,16},{8,24},{16,0},{24,8},{32,48},{40,56},{48,32},{56,40},{64,80... | collective-permute-start | bytes 466952 | tf_op jit(solution)/shard_map/ppermute | solution.py:18
  4.5 5.1 %collective-permute-start.4 = (bf16[152,512]{1,0:T(8,128)(2,1)}, bf16[152,512]{1,0:T(8,128)(2,1)S(1)}, u32[]{:S(2)}, u32[]{:S(2)}) collective-permute-start(bf16[152,512]{1,0:T(8,128)(2,1)} %rest_8_.1), channel_id=1, source_target_pairs={{0,32},{8,40},{16,48},{24,56},{32,0},{40,8},{48,16},{56,24},{64,96... | collective-permute-start | bytes 466952 | tf_op jit(solution)/shard_map/ppermute | solution.py:18
  9.6 0.6 pad_add_fusion.2.place_ref
  10.2 3.6 %upward.1 = f32[32,152]{1,0:T(8,128)} custom-call(s32[2]{0:T(128)} %pad_add_fusion.2.place_ref, bf16[152,512]{1,0:T(8,128)(2,1)} %rest_8_.1, bf16[8,152,152]{2,1,0:T(8,128)(2,1)} %up_ref.1), custom_call_target="tpu_custom_call" | custom-call | tf_op jit(solution)/shard_map/upward/pallas_call | solution.py:53
  13.8 1.2 collective-permute-start
  15.1 0.0 copy-start.2
  15.1 3.0 %relayout.8.rest_0_ = bf16[160,16,152]{2,1,0:T(8,128)(2,1)} custom-call(bf16[152,152,160]{2,1,0:T(8,128)(2,1)} %bitcast.7), custom_call_target="tpu_custom_call" | custom-call | flops 124518400 | bytes 2334720 | tf_op jit(solution)/shard_map/relayout/pallas_call | solution.py:91
  18.1 0.0 collective-permute-done
  18.1 0.0 copy-done.2
  18.1 0.0 copy-start
  18.1 1.4 %collective-permute-start.1 = (f32[32,152]{1,0:T(8,128)S(1)}, f32[32,152]{1,0:T(8,128)S(1)}, u32[]{:S(2)}, u32[]{:S(2)}) collective-permute-start(f32[32,152]{1,0:T(8,128)S(1)} %add.32), channel_id=1, source_target_pairs={{0,2},{1,3},{2,0},{3,1},{4,6},{5,7},{6,4},{7,5},{8,10},{9,11},{10,... | collective-permute-start | bytes 58376 | tf_op jit(solution)/shard_map/ppermute | solution.py:18
  19.5 3.0 %relayout.9.rest_1_ = bf16[160,16,152]{2,1,0:T(8,128)(2,1)} custom-call(bf16[152,152,160]{2,1,0:T(8,128)(2,1)} %bitcast.8), custom_call_target="tpu_custom_call" | custom-call | flops 124518400 | bytes 2334720 | tf_op jit(solution)/shard_map/relayout/pallas_call | solution.py:91
  22.5 0.0 collective-permute-done.1
  22.5 2.7 %collective-permute-start.2 = (f32[32,152]{1,0:T(8,128)S(1)}, f32[32,152]{1,0:T(8,128)S(1)}, u32[]{:S(2)}, u32[]{:S(2)}) collective-permute-start(f32[32,152]{1,0:T(8,128)S(1)} %add.33), channel_id=1, source_target_pairs={{0,4},{1,5},{2,6},{3,7},{4,0},{5,1},{6,2},{7,3},{8,12},{9,13},{10,... | collective-permute-start | bytes 58376 | tf_op jit(solution)/shard_map/ppermute | solution.py:18
  25.2 0.0 copy-done
  25.2 0.0 collective-permute-start.13
  25.2 1.1 collective-permute-start.11
  26.4 3.1 %relayout.10.rest_2_ = bf16[160,16,152]{2,1,0:T(8,128)(2,1)} custom-call(bf16[152,152,160]{2,1,0:T(8,128)(2,1)} %bitcast.9), custom_call_target="tpu_custom_call" | custom-call | flops 124518400 | bytes 2334720 | tf_op jit(solution)/shard_map/relayout/pallas_call | solution.py:91
  29.4 0.0 collective-permute-done.2
  29.5 0.0 copy-start.1
  29.5 0.0 copy-start.3
  29.5 0.8 collective-permute-start.3
  30.3 3.7 %relayout.11.rest_3_ = bf16[160,32,152]{2,1,0:T(8,128)(2,1)} custom-call(bf16[152,152,160]{2,1,0:T(8,128)(2,1)} %bitcast.10), custom_call_target="tpu_custom_call" | custom-call | flops 249036800 | bytes 4669440 | tf_op jit(solution)/shard_map/relayout/pallas_call | solution.py:91
  34.0 0.0 collective-permute-done.3
  34.0 2.7 %collective-permute-start.8 = (bf16[152,512]{1,0:T(8,128)(2,1)S(1)}, bf16[152,512]{1,0:T(8,128)(2,1)S(1)}, u32[]{:S(2)}, u32[]{:S(2)}) collective-permute-start(bf16[152,512]{1,0:T(8,128)(2,1)S(1)} %copy-done), channel_id=1, source_target_pairs={{0,128},{8,136},{16,144},{24,152},{32,160},{40,168},{48,176},{56,1... | collective-permute-start | bytes 466952 | tf_op jit(solution)/shard_map/ppermute | solution.py:18
  36.8 0.0 collective-permute-done.4.rest_14_
  36.8 0.8 collective-permute-start.7
  37.6 0.0 collective-permute-done.5.rest_13_
  37.6 1.2 collective-permute-start.6
  38.8 0.0 copy-done.1
  38.8 0.0 copy-done.3
  38.9 0.1 copy.11
  39.0 3.0 %relayout.12.rest_4_ = bf16[160,16,152]{2,1,0:T(8,128)(2,1)} custom-call(bf16[152,152,160]{2,1,0:T(8,128)(2,1)} %bitcast.11), custom_call_target="tpu_custom_call" | custom-call | flops 124518400 | bytes 2334720 | tf_op jit(solution)/shard_map/relayout/pallas_call | solution.py:91
  42.0 0.0 collective-permute-done.6
  42.0 0.3 collective-permute-start.10
  42.3 0.0 collective-permute-done.7.rest_12_
  42.3 3.2 %collective-permute-start.14 = (bf16[152,512]{1,0:T(8,128)(2,1)S(1)}, bf16[152,512]{1,0:T(8,128)(2,1)S(1)}, u32[]{:S(2)}, u32[]{:S(2)}) collective-permute-start(bf16[152,512]{1,0:T(8,128)(2,1)S(1)} %copy-done), channel_id=1, source_target_pairs={{0,1},{1,0},{2,3},{3,2},{4,5},{5,4},{6,7},{7,6},{8,9},{9,8},{10,11... | collective-permute-start | bytes 466952 | tf_op jit(solution)/shard_map/ppermute | solution.py:18
  45.5 0.0 collective-permute-done.8.rest_16_
  45.5 1.2 collective-permute-start.9
  46.7 3.0 %relayout.13.rest_5_ = bf16[160,16,152]{2,1,0:T(8,128)(2,1)} custom-call(bf16[152,152,160]{2,1,0:T(8,128)(2,1)} %bitcast.12), custom_call_target="tpu_custom_call" | custom-call | flops 124518400 | bytes 2334720 | tf_op jit(solution)/shard_map/relayout/pallas_call | solution.py:91
  49.6 0.0 collective-permute-done.9
  49.7 0.0 collective-permute-done.10.rest_15_
  49.7 0.0 collective-permute-done.11.rest_11_
  49.7 0.8 collective-permute-start.12
  50.5 0.0 copy-start.4
  50.6 3.0 %relayout.14.rest_6_ = bf16[160,16,152]{2,1,0:T(8,128)(2,1)} custom-call(bf16[152,152,160]{2,1,0:T(8,128)(2,1)} %bitcast.13), custom_call_target="tpu_custom_call" | custom-call | flops 124518400 | bytes 2334720 | tf_op jit(solution)/shard_map/relayout/pallas_call | solution.py:91
  53.6 0.6 collective-permute-done.12
  54.2 0.0 collective-permute-done.13.rest_10_
  54.2 0.0 collective-permute-done.14.rest_9_
  54.2 0.5 collective-permute-start.15
  54.8 0.0 copy-done.4
  54.8 0.1 copy.13.slots_ref
  54.9 3.5 %relayout.15.rest_7_ = bf16[160,24,152]{2,1,0:T(8,128)(2,1)} custom-call(bf16[152,152,160]{2,1,0:T(8,128)(2,1)} %bitcast.14), custom_call_target="tpu_custom_call" | custom-call | flops 186777600 | bytes 3502080 | tf_op jit(solution)/shard_map/relayout/pallas_call | solution.py:91
  58.4 2.6 %collective-permute-done.15 = f32[32,152]{1,0:T(8,128)S(1)} collective-permute-done((f32[32,152]{1,0:T(8,128)S(1)}, f32[32,152]{1,0:T(8,128)S(1)}, u32[]{:S(2)}, u32[]{:S(2)}) %collective-permute-start.15) | collective-permute-done | bytes 19488 | tf_op jit(solution)/shard_map/ppermute | solution.py:18
  61.0 65.2 %translate.1 = (f32[152,512]{1,0:T(8,128)}, f32[32,152]{1,0:T(8,128)}) custom-call(s32[160,544]{1,0:T(8,128)S(1)} %pad_add_fusion.idx_hbm, s32[512,9]{1,0:T(8,128)S(1)} %copy.13.slots_ref, f32[32,152]{1,0:T(8,128)S(1)} %add.39.coarse_ref, bf16[160,16,152]{2,1,0:T(8,128)(2,1)} %relayout.8.rest_0_, bf16[160,16,152]{2,1,0:T(8,128)(2,1)} %relayout.9.rest_1_, ...), custom_call_target="tpu_custom_call" | custom-call | tf_op jit(solution)/shard_map/translate/pallas_call | solution.py:219
  (13 shorter events, 0.1 us)
Async XLA Ops:
  0.6 37.0 %collective-permute-start.5 = (bf16[152,512]{1,0:T(8,128)(2,1)}, bf16[152,512]{1,0:T(8,128)(2,1)S(1)}, u32[]{:S(2)}, u32[]{:S(2)}) collective-permute-start(bf16[152,512]{1,0:T(8,128)(2,1)} %rest_8_.1), channel_id=1, source_target_pairs={{0,16},{8,24},{16,0},{24,8},{32,48},{40,56},{48,32},{56,40},{64,80... | collective-permute-start | bytes 466952 | tf_op jit(solution)/shard_map/ppermute | solution.py:18
  4.5 32.3 %collective-permute-start.4 = (bf16[152,512]{1,0:T(8,128)(2,1)}, bf16[152,512]{1,0:T(8,128)(2,1)S(1)}, u32[]{:S(2)}, u32[]{:S(2)}) collective-permute-start(bf16[152,512]{1,0:T(8,128)(2,1)} %rest_8_.1), channel_id=1, source_target_pairs={{0,32},{8,40},{16,48},{24,56},{32,0},{40,8},{48,16},{56,24},{64,96... | collective-permute-start | bytes 466952 | tf_op jit(solution)/shard_map/ppermute | solution.py:18
  13.8 4.3 %collective-permute-start = (f32[32,152]{1,0:T(8,128)}, f32[32,152]{1,0:T(8,128)S(1)}, u32[]{:S(2)}, u32[]{:S(2)}) collective-permute-start(f32[32,152]{1,0:T(8,128)} %upward.1), channel_id=1, source_target_pairs={{0,1},{1,0},{2,3},{3,2},{4,5},{5,4},{6,7},{7,6},{8,9},{9,8},{10,11... | collective-permute-start | bytes 58376 | tf_op jit(solution)/shard_map/ppermute | solution.py:18
  15.1 3.0 %copy-start.2 = (f32[32,152]{1,0:T(8,128)S(1)}, f32[32,152]{1,0:T(8,128)}, u32[]{:S(2)}) copy-start(f32[32,152]{1,0:T(8,128)} %upward.1) | copy-start | bytes 58372
  18.1 7.1 %copy-start = (bf16[152,512]{1,0:T(8,128)(2,1)S(1)}, bf16[152,512]{1,0:T(8,128)(2,1)}, u32[]{:S(2)}) copy-start(bf16[152,512]{1,0:T(8,128)(2,1)} %rest_8_.1) | copy-start | bytes 466948
  18.1 4.4 %collective-permute-start.1 = (f32[32,152]{1,0:T(8,128)S(1)}, f32[32,152]{1,0:T(8,128)S(1)}, u32[]{:S(2)}, u32[]{:S(2)}) collective-permute-start(f32[32,152]{1,0:T(8,128)S(1)} %add.32), channel_id=1, source_target_pairs={{0,2},{1,3},{2,0},{3,1},{4,6},{5,7},{6,4},{7,5},{8,10},{9,11},{10,... | collective-permute-start | bytes 58376 | tf_op jit(solution)/shard_map/ppermute | solution.py:18
  22.5 6.9 %collective-permute-start.2 = (f32[32,152]{1,0:T(8,128)S(1)}, f32[32,152]{1,0:T(8,128)S(1)}, u32[]{:S(2)}, u32[]{:S(2)}) collective-permute-start(f32[32,152]{1,0:T(8,128)S(1)} %add.33), channel_id=1, source_target_pairs={{0,4},{1,5},{2,6},{3,7},{4,0},{5,1},{6,2},{7,3},{8,12},{9,13},{10,... | collective-permute-start | bytes 58376 | tf_op jit(solution)/shard_map/ppermute | solution.py:18
  25.2 29.0 %collective-permute-start.13 = (bf16[152,512]{1,0:T(8,128)(2,1)S(1)}, bf16[152,512]{1,0:T(8,128)(2,1)S(1)}, u32[]{:S(2)}, u32[]{:S(2)}) collective-permute-start(bf16[152,512]{1,0:T(8,128)(2,1)S(1)} %copy-done), channel_id=1, source_target_pairs={{0,2},{1,3},{2,0},{3,1},{4,6},{5,7},{6,4},{7,5},{8,10},{9,11},{10,... | collective-permute-start | bytes 466952 | tf_op jit(solution)/shard_map/ppermute | solution.py:18
  25.2 24.4 %collective-permute-start.11 = (bf16[152,512]{1,0:T(8,128)(2,1)S(1)}, bf16[152,512]{1,0:T(8,128)(2,1)S(1)}, u32[]{:S(2)}, u32[]{:S(2)}) collective-permute-start(bf16[152,512]{1,0:T(8,128)(2,1)S(1)} %copy-done), channel_id=1, source_target_pairs={{0,4},{1,5},{2,6},{3,7},{4,0},{5,1},{6,2},{7,3},{8,12},{9,13},{10,... | collective-permute-start | bytes 466952 | tf_op jit(solution)/shard_map/ppermute | solution.py:18
  29.5 9.3 %copy-start.1 = (s32[160,512]{1,0:T(8,128)S(1)}, s32[160,512]{1,0:T(8,128)}, u32[]{:S(2)}) copy-start(s32[160,512]{1,0:T(8,128)} %param.9) | copy-start | bytes 983044
  29.5 9.4 %copy-start.3 = (s32[160,32]{0,1:T(8,128)S(1)}, s32[160,32]{0,1:T(8,128)}, u32[]{:S(2)}) copy-start(s32[160,32]{0,1:T(8,128)} %param.11) | copy-start | bytes 61444
  29.5 4.6 %collective-permute-start.3 = (f32[32,152]{1,0:T(8,128)S(1)}, f32[32,152]{1,0:T(8,128)S(1)}, u32[]{:S(2)}, u32[]{:S(2)}) collective-permute-start(f32[32,152]{1,0:T(8,128)S(1)} %add.34), channel_id=1, source_target_pairs={{0,8},{8,0},{16,24},{24,16},{32,40},{40,32},{48,56},{56,48},{64,72... | collective-permute-start | bytes 58376 | tf_op jit(solution)/shard_map/ppermute | solution.py:18
  34.0 11.4 %collective-permute-start.8 = (bf16[152,512]{1,0:T(8,128)(2,1)S(1)}, bf16[152,512]{1,0:T(8,128)(2,1)S(1)}, u32[]{:S(2)}, u32[]{:S(2)}) collective-permute-start(bf16[152,512]{1,0:T(8,128)(2,1)S(1)} %copy-done), channel_id=1, source_target_pairs={{0,128},{8,136},{16,144},{24,152},{32,160},{40,168},{48,176},{56,1... | collective-permute-start | bytes 466952 | tf_op jit(solution)/shard_map/ppermute | solution.py:18
  36.8 5.5 %collective-permute-start.7 = (bf16[152,512]{1,0:T(8,128)(2,1)S(1)}, bf16[152,512]{1,0:T(8,128)(2,1)S(1)}, u32[]{:S(2)}, u32[]{:S(2)}) collective-permute-start(bf16[152,512]{1,0:T(8,128)(2,1)S(1)} %copy-done), channel_id=1, source_target_pairs={{0,8},{8,0},{16,24},{24,16},{32,40},{40,32},{48,56},{56,48},{64,72... | collective-permute-start | bytes 466952 | tf_op jit(solution)/shard_map/ppermute | solution.py:18
  37.6 4.4 %collective-permute-start.6 = (f32[32,152]{1,0:T(8,128)S(1)}, f32[32,152]{1,0:T(8,128)S(1)}, u32[]{:S(2)}, u32[]{:S(2)}) collective-permute-start(f32[32,152]{1,0:T(8,128)S(1)} %add.35), channel_id=1, source_target_pairs={{0,16},{8,24},{16,0},{24,8},{32,48},{40,56},{48,32},{56,40},{64,80... | collective-permute-start | bytes 58376 | tf_op jit(solution)/shard_map/ppermute | solution.py:18
  42.0 7.7 %collective-permute-start.10 = (bf16[152,512]{1,0:T(8,128)(2,1)S(1)}, bf16[152,512]{1,0:T(8,128)(2,1)S(1)}, u32[]{:S(2)}, u32[]{:S(2)}) collective-permute-start(bf16[152,512]{1,0:T(8,128)(2,1)S(1)} %copy-done), channel_id=1, source_target_pairs={{0,64},{8,72},{16,80},{24,88},{32,96},{40,104},{48,112},{56,120},{... | collective-permute-start | bytes 466952 | tf_op jit(solution)/shard_map/ppermute | solution.py:18
  42.3 11.9 %collective-permute-start.14 = (bf16[152,512]{1,0:T(8,128)(2,1)S(1)}, bf16[152,512]{1,0:T(8,128)(2,1)S(1)}, u32[]{:S(2)}, u32[]{:S(2)}) collective-permute-start(bf16[152,512]{1,0:T(8,128)(2,1)S(1)} %copy-done), channel_id=1, source_target_pairs={{0,1},{1,0},{2,3},{3,2},{4,5},{5,4},{6,7},{7,6},{8,9},{9,8},{10,11... | collective-permute-start | bytes 466952 | tf_op jit(solution)/shard_map/ppermute | solution.py:18
  45.5 4.2 %collective-permute-start.9 = (f32[32,152]{1,0:T(8,128)S(1)}, f32[32,152]{1,0:T(8,128)S(1)}, u32[]{:S(2)}, u32[]{:S(2)}) collective-permute-start(f32[32,152]{1,0:T(8,128)S(1)} %add.36), channel_id=1, source_target_pairs={{0,64},{8,72},{16,80},{24,88},{32,96},{40,104},{48,112},{56,120},{... | collective-permute-start | bytes 58376 | tf_op jit(solution)/shard_map/ppermute | solution.py:18
  49.7 4.5 %collective-permute-start.12 = (f32[32,152]{1,0:T(8,128)S(1)}, f32[32,152]{1,0:T(8,128)S(1)}, u32[]{:S(2)}, u32[]{:S(2)}) collective-permute-start(f32[32,152]{1,0:T(8,128)S(1)} %add.37), channel_id=1, source_target_pairs={{0,128},{8,136},{16,144},{24,152},{32,160},{40,168},{48,176},{56,1... | collective-permute-start | bytes 58376 | tf_op jit(solution)/shard_map/ppermute | solution.py:18
  50.5 4.2 %copy-start.4 = (s32[1,8,512]{2,1,0:T(8,128)S(1)}, s32[1,8,512]{2,1,0:T(8,128)}, u32[]{:S(2)}) copy-start(s32[1,8,512]{2,1,0:T(8,128)} %param.10) | copy-start | bytes 49156
  54.2 6.8 %collective-permute-start.15 = (f32[32,152]{1,0:T(8,128)S(1)}, f32[32,152]{1,0:T(8,128)S(1)}, u32[]{:S(2)}, u32[]{:S(2)}) collective-permute-start(f32[32,152]{1,0:T(8,128)S(1)} %add.38), channel_id=1, source_target_pairs={{0,32},{8,40},{16,48},{24,56},{32,0},{40,8},{48,16},{56,24},{64,96... | collective-permute-start | bytes 58376 | tf_op jit(solution)/shard_map/ppermute | solution.py:18

commit v6 on v5

--- a/solution.py
+++ b/solution.py
@@ -63,7 +63,7 @@
 SETTLED = 3
 STRIP = 16
 GROUP = 2
-PHASES = 8
+PHASES = 16
 CHUNKS = 2
 
 

time: 128 us -> 128 us (level)
  no operation moved by 1% of the time
where the time goes in v6:
time: 128 us; the launch traced here: 126 us
  Pallas kernels  93.8 us (73%)
  starting transfers between devices  26.8 us (21%)
  waiting for transfers between devices  3.25 us (3%)
    pallas_call x1, Pallas kernels, translate(): pl.pallas_call(functools.partial(translate_kernel, sections, len(far_piec...  64.8 us
    ppermute x16, starting transfers between devices, from_partner(): return lax.ppermute(value, axis, pairs)  26.8 us
    pallas_call x8, Pallas kernels, relayout(): pl.pallas_call(relayout_kernel, grid=(strips,), in_specs=[pl.BlockSpec((S...  25.4 us
    pallas_call x1, Pallas kernels, upward(): pl.pallas_call(upward_kernel, in_specs=[pl.BlockSpec(memory_space=pltpu.S...  3.58 us
    ppermute x16, waiting for transfers between devices, from_partner(): return lax.ppermute(value, axis, pairs)  3.25 us
  transfers between devices with their start and end apart: 16, of which 2 were waited for; matrix products, arithmetic and copies ran while one was open for 1% of the time, Pallas kernels for 23%

profile of v6, /device:TPU:1, one launch (start us, length us, event | category | flops | bytes accessed | tf_op | source)
XLA Modules:
  0.0 125.8 jit_solution(483696119503353707)
XLA Ops:
  0.6 3.9 %collective-permute-start.5 = (bf16[152,512]{1,0:T(8,128)(2,1)}, bf16[152,512]{1,0:T(8,128)(2,1)S(1)}, u32[]{:S(2)}, u32[]{:S(2)}) collective-permute-start(bf16[152,512]{1,0:T(8,128)(2,1)} %rest_8_.1), channel_id=1, source_target_pairs={{0,16},{8,24},{16,0},{24,8},{32,48},{40,56},{48,32},{56,40},{64,80... | collective-permute-start | bytes 466952 | tf_op jit(solution)/shard_map/ppermute | solution.py:18
  4.5 5.1 %collective-permute-start.4 = (bf16[152,512]{1,0:T(8,128)(2,1)}, bf16[152,512]{1,0:T(8,128)(2,1)S(1)}, u32[]{:S(2)}, u32[]{:S(2)}) collective-permute-start(bf16[152,512]{1,0:T(8,128)(2,1)} %rest_8_.1), channel_id=1, source_target_pairs={{0,32},{8,40},{16,48},{24,56},{32,0},{40,8},{48,16},{56,24},{64,96... | collective-permute-start | bytes 466952 | tf_op jit(solution)/shard_map/ppermute | solution.py:18
  9.6 0.6 pad_add_fusion.2.place_ref
  10.2 3.6 %upward.1 = f32[32,152]{1,0:T(8,128)} custom-call(s32[2]{0:T(128)} %pad_add_fusion.2.place_ref, bf16[152,512]{1,0:T(8,128)(2,1)} %rest_8_.1, bf16[8,152,152]{2,1,0:T(8,128)(2,1)} %up_ref.1), custom_call_target="tpu_custom_call" | custom-call | tf_op jit(solution)/shard_map/upward/pallas_call | solution.py:53
  13.8 1.2 collective-permute-start
  15.1 0.0 copy-start.2
  15.1 3.0 %relayout.8.rest_0_ = bf16[160,16,152]{2,1,0:T(8,128)(2,1)} custom-call(bf16[152,152,160]{2,1,0:T(8,128)(2,1)} %bitcast.7), custom_call_target="tpu_custom_call" | custom-call | flops 124518400 | bytes 2334720 | tf_op jit(solution)/shard_map/relayout/pallas_call | solution.py:91
  18.1 0.0 collective-permute-done
  18.1 0.0 copy-done.2
  18.1 0.0 copy-start
  18.1 1.4 %collective-permute-start.1 = (f32[32,152]{1,0:T(8,128)S(1)}, f32[32,152]{1,0:T(8,128)S(1)}, u32[]{:S(2)}, u32[]{:S(2)}) collective-permute-start(f32[32,152]{1,0:T(8,128)S(1)} %add.32), channel_id=1, source_target_pairs={{0,2},{1,3},{2,0},{3,1},{4,6},{5,7},{6,4},{7,5},{8,10},{9,11},{10,... | collective-permute-start | bytes 58376 | tf_op jit(solution)/shard_map/ppermute | solution.py:18
  19.5 3.0 %relayout.9.rest_1_ = bf16[160,16,152]{2,1,0:T(8,128)(2,1)} custom-call(bf16[152,152,160]{2,1,0:T(8,128)(2,1)} %bitcast.8), custom_call_target="tpu_custom_call" | custom-call | flops 124518400 | bytes 2334720 | tf_op jit(solution)/shard_map/relayout/pallas_call | solution.py:91
  22.5 0.0 collective-permute-done.1
  22.5 2.7 %collective-permute-start.2 = (f32[32,152]{1,0:T(8,128)S(1)}, f32[32,152]{1,0:T(8,128)S(1)}, u32[]{:S(2)}, u32[]{:S(2)}) collective-permute-start(f32[32,152]{1,0:T(8,128)S(1)} %add.33), channel_id=1, source_target_pairs={{0,4},{1,5},{2,6},{3,7},{4,0},{5,1},{6,2},{7,3},{8,12},{9,13},{10,... | collective-permute-start | bytes 58376 | tf_op jit(solution)/shard_map/ppermute | solution.py:18
  25.2 0.0 copy-done
  25.2 0.0 collective-permute-start.13
  25.2 1.1 collective-permute-start.11
  26.4 3.1 %relayout.10.rest_2_ = bf16[160,16,152]{2,1,0:T(8,128)(2,1)} custom-call(bf16[152,152,160]{2,1,0:T(8,128)(2,1)} %bitcast.9), custom_call_target="tpu_custom_call" | custom-call | flops 124518400 | bytes 2334720 | tf_op jit(solution)/shard_map/relayout/pallas_call | solution.py:91
  29.4 0.0 collective-permute-done.2
  29.5 0.0 copy-start.1
  29.5 0.0 copy-start.3
  29.5 0.8 collective-permute-start.3
  30.3 3.7 %relayout.11.rest_3_ = bf16[160,32,152]{2,1,0:T(8,128)(2,1)} custom-call(bf16[152,152,160]{2,1,0:T(8,128)(2,1)} %bitcast.10), custom_call_target="tpu_custom_call" | custom-call | flops 249036800 | bytes 4669440 | tf_op jit(solution)/shard_map/relayout/pallas_call | solution.py:91
  34.0 0.0 collective-permute-done.3
  34.0 2.7 %collective-permute-start.8 = (bf16[152,512]{1,0:T(8,128)(2,1)S(1)}, bf16[152,512]{1,0:T(8,128)(2,1)S(1)}, u32[]{:S(2)}, u32[]{:S(2)}) collective-permute-start(bf16[152,512]{1,0:T(8,128)(2,1)S(1)} %copy-done), channel_id=1, source_target_pairs={{0,128},{8,136},{16,144},{24,152},{32,160},{40,168},{48,176},{56,1... | collective-permute-start | bytes 466952 | tf_op jit(solution)/shard_map/ppermute | solution.py:18
  36.8 0.0 collective-permute-done.4.rest_14_
  36.8 0.8 collective-permute-start.7
  37.6 0.0 collective-permute-done.5.rest_13_
  37.6 1.2 collective-permute-start.6
  38.8 0.0 copy-done.1
  38.8 0.0 copy-done.3
  38.9 0.1 copy.11
  39.0 3.0 %relayout.12.rest_4_ = bf16[160,16,152]{2,1,0:T(8,128)(2,1)} custom-call(bf16[152,152,160]{2,1,0:T(8,128)(2,1)} %bitcast.11), custom_call_target="tpu_custom_call" | custom-call | flops 124518400 | bytes 2334720 | tf_op jit(solution)/shard_map/relayout/pallas_call | solution.py:91
  42.0 0.0 collective-permute-done.6
  42.0 0.3 collective-permute-start.10
  42.3 0.0 collective-permute-done.7.rest_12_
  42.3 3.2 %collective-permute-start.14 = (bf16[152,512]{1,0:T(8,128)(2,1)S(1)}, bf16[152,512]{1,0:T(8,128)(2,1)S(1)}, u32[]{:S(2)}, u32[]{:S(2)}) collective-permute-start(bf16[152,512]{1,0:T(8,128)(2,1)S(1)} %copy-done), channel_id=1, source_target_pairs={{0,1},{1,0},{2,3},{3,2},{4,5},{5,4},{6,7},{7,6},{8,9},{9,8},{10,11... | collective-permute-start | bytes 466952 | tf_op jit(solution)/shard_map/ppermute | solution.py:18
  45.5 0.0 collective-permute-done.8.rest_16_
  45.5 1.2 collective-permute-start.9
  46.7 3.0 %relayout.13.rest_5_ = bf16[160,16,152]{2,1,0:T(8,128)(2,1)} custom-call(bf16[152,152,160]{2,1,0:T(8,128)(2,1)} %bitcast.12), custom_call_target="tpu_custom_call" | custom-call | flops 124518400 | bytes 2334720 | tf_op jit(solution)/shard_map/relayout/pallas_call | solution.py:91
  49.6 0.0 collective-permute-done.9
  49.7 0.0 collective-permute-done.10.rest_15_
  49.7 0.0 collective-permute-done.11.rest_11_
  49.7 0.6 collective-permute-start.12
  50.4 0.0 copy-start.4
  50.4 3.0 %relayout.14.rest_6_ = bf16[160,16,152]{2,1,0:T(8,128)(2,1)} custom-call(bf16[152,152,160]{2,1,0:T(8,128)(2,1)} %bitcast.13), custom_call_target="tpu_custom_call" | custom-call | flops 124518400 | bytes 2334720 | tf_op jit(solution)/shard_map/relayout/pallas_call | solution.py:91
  53.4 0.7 collective-permute-done.12
  54.0 0.0 collective-permute-done.13.rest_10_
  54.0 0.0 collective-permute-done.14.rest_9_
  54.1 0.5 collective-permute-start.15
  54.6 0.0 copy-done.4
  54.6 0.1 copy.13.slots_ref
  54.7 3.5 %relayout.15.rest_7_ = bf16[160,24,152]{2,1,0:T(8,128)(2,1)} custom-call(bf16[152,152,160]{2,1,0:T(8,128)(2,1)} %bitcast.14), custom_call_target="tpu_custom_call" | custom-call | flops 186777600 | bytes 3502080 | tf_op jit(solution)/shard_map/relayout/pallas_call | solution.py:91
  58.3 2.6 %collective-permute-done.15 = f32[32,152]{1,0:T(8,128)S(1)} collective-permute-done((f32[32,152]{1,0:T(8,128)S(1)}, f32[32,152]{1,0:T(8,128)S(1)}, u32[]{:S(2)}, u32[]{:S(2)}) %collective-permute-start.15) | collective-permute-done | bytes 19488 | tf_op jit(solution)/shard_map/ppermute | solution.py:18
  60.8 64.8 %translate.1 = (f32[152,512]{1,0:T(8,128)}, f32[32,152]{1,0:T(8,128)}) custom-call(s32[160,544]{1,0:T(8,128)S(1)} %pad_add_fusion.idx_hbm, s32[512,9]{1,0:T(8,128)S(1)} %copy.13.slots_ref, f32[32,152]{1,0:T(8,128)S(1)} %add.39.coarse_ref, bf16[160,16,152]{2,1,0:T(8,128)(2,1)} %relayout.8.rest_0_, bf16[160,16,152]{2,1,0:T(8,128)(2,1)} %relayout.9.rest_1_, ...), custom_call_target="tpu_custom_call" | custom-call | tf_op jit(solution)/shard_map/translate/pallas_call | solution.py:219
  (13 shorter events, 0.1 us)
Async XLA Ops:
  0.6 37.0 %collective-permute-start.5 = (bf16[152,512]{1,0:T(8,128)(2,1)}, bf16[152,512]{1,0:T(8,128)(2,1)S(1)}, u32[]{:S(2)}, u32[]{:S(2)}) collective-permute-start(bf16[152,512]{1,0:T(8,128)(2,1)} %rest_8_.1), channel_id=1, source_target_pairs={{0,16},{8,24},{16,0},{24,8},{32,48},{40,56},{48,32},{56,40},{64,80... | collective-permute-start | bytes 466952 | tf_op jit(solution)/shard_map/ppermute | solution.py:18
  4.5 32.3 %collective-permute-start.4 = (bf16[152,512]{1,0:T(8,128)(2,1)}, bf16[152,512]{1,0:T(8,128)(2,1)S(1)}, u32[]{:S(2)}, u32[]{:S(2)}) collective-permute-start(bf16[152,512]{1,0:T(8,128)(2,1)} %rest_8_.1), channel_id=1, source_target_pairs={{0,32},{8,40},{16,48},{24,56},{32,0},{40,8},{48,16},{56,24},{64,96... | collective-permute-start | bytes 466952 | tf_op jit(solution)/shard_map/ppermute | solution.py:18
  13.8 4.3 %collective-permute-start = (f32[32,152]{1,0:T(8,128)}, f32[32,152]{1,0:T(8,128)S(1)}, u32[]{:S(2)}, u32[]{:S(2)}) collective-permute-start(f32[32,152]{1,0:T(8,128)} %upward.1), channel_id=1, source_target_pairs={{0,1},{1,0},{2,3},{3,2},{4,5},{5,4},{6,7},{7,6},{8,9},{9,8},{10,11... | collective-permute-start | bytes 58376 | tf_op jit(solution)/shard_map/ppermute | solution.py:18
  15.1 3.0 %copy-start.2 = (f32[32,152]{1,0:T(8,128)S(1)}, f32[32,152]{1,0:T(8,128)}, u32[]{:S(2)}) copy-start(f32[32,152]{1,0:T(8,128)} %upward.1) | copy-start | bytes 58372
  18.1 7.1 %copy-start = (bf16[152,512]{1,0:T(8,128)(2,1)S(1)}, bf16[152,512]{1,0:T(8,128)(2,1)}, u32[]{:S(2)}) copy-start(bf16[152,512]{1,0:T(8,128)(2,1)} %rest_8_.1) | copy-start | bytes 466948
  18.1 4.4 %collective-permute-start.1 = (f32[32,152]{1,0:T(8,128)S(1)}, f32[32,152]{1,0:T(8,128)S(1)}, u32[]{:S(2)}, u32[]{:S(2)}) collective-permute-start(f32[32,152]{1,0:T(8,128)S(1)} %add.32), channel_id=1, source_target_pairs={{0,2},{1,3},{2,0},{3,1},{4,6},{5,7},{6,4},{7,5},{8,10},{9,11},{10,... | collective-permute-start | bytes 58376 | tf_op jit(solution)/shard_map/ppermute | solution.py:18
  22.5 6.9 %collective-permute-start.2 = (f32[32,152]{1,0:T(8,128)S(1)}, f32[32,152]{1,0:T(8,128)S(1)}, u32[]{:S(2)}, u32[]{:S(2)}) collective-permute-start(f32[32,152]{1,0:T(8,128)S(1)} %add.33), channel_id=1, source_target_pairs={{0,4},{1,5},{2,6},{3,7},{4,0},{5,1},{6,2},{7,3},{8,12},{9,13},{10,... | collective-permute-start | bytes 58376 | tf_op jit(solution)/shard_map/ppermute | solution.py:18
  25.2 28.8 %collective-permute-start.13 = (bf16[152,512]{1,0:T(8,128)(2,1)S(1)}, bf16[152,512]{1,0:T(8,128)(2,1)S(1)}, u32[]{:S(2)}, u32[]{:S(2)}) collective-permute-start(bf16[152,512]{1,0:T(8,128)(2,1)S(1)} %copy-done), channel_id=1, source_target_pairs={{0,2},{1,3},{2,0},{3,1},{4,6},{5,7},{6,4},{7,5},{8,10},{9,11},{10,... | collective-permute-start | bytes 466952 | tf_op jit(solution)/shard_map/ppermute | solution.py:18
  25.2 24.4 %collective-permute-start.11 = (bf16[152,512]{1,0:T(8,128)(2,1)S(1)}, bf16[152,512]{1,0:T(8,128)(2,1)S(1)}, u32[]{:S(2)}, u32[]{:S(2)}) collective-permute-start(bf16[152,512]{1,0:T(8,128)(2,1)S(1)} %copy-done), channel_id=1, source_target_pairs={{0,4},{1,5},{2,6},{3,7},{4,0},{5,1},{6,2},{7,3},{8,12},{9,13},{10,... | collective-permute-start | bytes 466952 | tf_op jit(solution)/shard_map/ppermute | solution.py:18
  29.5 9.3 %copy-start.1 = (s32[160,512]{1,0:T(8,128)S(1)}, s32[160,512]{1,0:T(8,128)}, u32[]{:S(2)}) copy-start(s32[160,512]{1,0:T(8,128)} %param.9) | copy-start | bytes 983044
  29.5 9.4 %copy-start.3 = (s32[160,32]{0,1:T(8,128)S(1)}, s32[160,32]{0,1:T(8,128)}, u32[]{:S(2)}) copy-start(s32[160,32]{0,1:T(8,128)} %param.11) | copy-start | bytes 61444
  29.5 4.6 %collective-permute-start.3 = (f32[32,152]{1,0:T(8,128)S(1)}, f32[32,152]{1,0:T(8,128)S(1)}, u32[]{:S(2)}, u32[]{:S(2)}) collective-permute-start(f32[32,152]{1,0:T(8,128)S(1)} %add.34), channel_id=1, source_target_pairs={{0,8},{8,0},{16,24},{24,16},{32,40},{40,32},{48,56},{56,48},{64,72... | collective-permute-start | bytes 58376 | tf_op jit(solution)/shard_map/ppermute | solution.py:18
  34.0 11.4 %collective-permute-start.8 = (bf16[152,512]{1,0:T(8,128)(2,1)S(1)}, bf16[152,512]{1,0:T(8,128)(2,1)S(1)}, u32[]{:S(2)}, u32[]{:S(2)}) collective-permute-start(bf16[152,512]{1,0:T(8,128)(2,1)S(1)} %copy-done), channel_id=1, source_target_pairs={{0,128},{8,136},{16,144},{24,152},{32,160},{40,168},{48,176},{56,1... | collective-permute-start | bytes 466952 | tf_op jit(solution)/shard_map/ppermute | solution.py:18
  36.8 5.5 %collective-permute-start.7 = (bf16[152,512]{1,0:T(8,128)(2,1)S(1)}, bf16[152,512]{1,0:T(8,128)(2,1)S(1)}, u32[]{:S(2)}, u32[]{:S(2)}) collective-permute-start(bf16[152,512]{1,0:T(8,128)(2,1)S(1)} %copy-done), channel_id=1, source_target_pairs={{0,8},{8,0},{16,24},{24,16},{32,40},{40,32},{48,56},{56,48},{64,72... | collective-permute-start | bytes 466952 | tf_op jit(solution)/shard_map/ppermute | solution.py:18
  37.6 4.4 %collective-permute-start.6 = (f32[32,152]{1,0:T(8,128)S(1)}, f32[32,152]{1,0:T(8,128)S(1)}, u32[]{:S(2)}, u32[]{:S(2)}) collective-permute-start(f32[32,152]{1,0:T(8,128)S(1)} %add.35), channel_id=1, source_target_pairs={{0,16},{8,24},{16,0},{24,8},{32,48},{40,56},{48,32},{56,40},{64,80... | collective-permute-start | bytes 58376 | tf_op jit(solution)/shard_map/ppermute | solution.py:18
  42.0 7.7 %collective-permute-start.10 = (bf16[152,512]{1,0:T(8,128)(2,1)S(1)}, bf16[152,512]{1,0:T(8,128)(2,1)S(1)}, u32[]{:S(2)}, u32[]{:S(2)}) collective-permute-start(bf16[152,512]{1,0:T(8,128)(2,1)S(1)} %copy-done), channel_id=1, source_target_pairs={{0,64},{8,72},{16,80},{24,88},{32,96},{40,104},{48,112},{56,120},{... | collective-permute-start | bytes 466952 | tf_op jit(solution)/shard_map/ppermute | solution.py:18
  42.3 11.7 %collective-permute-start.14 = (bf16[152,512]{1,0:T(8,128)(2,1)S(1)}, bf16[152,512]{1,0:T(8,128)(2,1)S(1)}, u32[]{:S(2)}, u32[]{:S(2)}) collective-permute-start(bf16[152,512]{1,0:T(8,128)(2,1)S(1)} %copy-done), channel_id=1, source_target_pairs={{0,1},{1,0},{2,3},{3,2},{4,5},{5,4},{6,7},{7,6},{8,9},{9,8},{10,11... | collective-permute-start | bytes 466952 | tf_op jit(solution)/shard_map/ppermute | solution.py:18
  45.5 4.2 %collective-permute-start.9 = (f32[32,152]{1,0:T(8,128)S(1)}, f32[32,152]{1,0:T(8,128)S(1)}, u32[]{:S(2)}, u32[]{:S(2)}) collective-permute-start(f32[32,152]{1,0:T(8,128)S(1)} %add.36), channel_id=1, source_target_pairs={{0,64},{8,72},{16,80},{24,88},{32,96},{40,104},{48,112},{56,120},{... | collective-permute-start | bytes 58376 | tf_op jit(solution)/shard_map/ppermute | solution.py:18
  49.7 4.4 %collective-permute-start.12 = (f32[32,152]{1,0:T(8,128)S(1)}, f32[32,152]{1,0:T(8,128)S(1)}, u32[]{:S(2)}, u32[]{:S(2)}) collective-permute-start(f32[32,152]{1,0:T(8,128)S(1)} %add.37), channel_id=1, source_target_pairs={{0,128},{8,136},{16,144},{24,152},{32,160},{40,168},{48,176},{56,1... | collective-permute-start | bytes 58376 | tf_op jit(solution)/shard_map/ppermute | solution.py:18
  50.4 4.2 %copy-start.4 = (s32[1,8,512]{2,1,0:T(8,128)S(1)}, s32[1,8,512]{2,1,0:T(8,128)}, u32[]{:S(2)}) copy-start(s32[1,8,512]{2,1,0:T(8,128)} %param.10) | copy-start | bytes 49156
  54.1 6.8 %collective-permute-start.15 = (f32[32,152]{1,0:T(8,128)S(1)}, f32[32,152]{1,0:T(8,128)S(1)}, u32[]{:S(2)}, u32[]{:S(2)}) collective-permute-start(f32[32,152]{1,0:T(8,128)S(1)} %add.38), channel_id=1, source_target_pairs={{0,32},{8,40},{16,48},{24,56},{32,0},{40,8},{48,16},{56,24},{64,96... | collective-permute-start | bytes 58376 | tf_op jit(solution)/shard_map/ppermute | solution.py:18
